TPU v7x, 32 devices: a whole 2x2x4 slice. The times are simulated.
32 devices in a mesh: grp: 1, row: 8 (over z, y), br: 2 (over core), pb: 2 (over x).
Axes of the slice: x: 2, y: 2, z: 4, core: 2. Of those that a mesh axis runs over, the one named last changes fastest.
Arguments:
- homolog_representation: bfloat16 [128, 64, 256], P(('grp', 'pb'), ('row', 'br')), may hold values from -6 to 6
- pair_state: bfloat16 [64, 64, 128], P(('grp', 'row', 'br'), 'pb'), may hold values from -6 to 6
- genuine_chain_indicator: int32 [128], P('grp'), may hold values from 0 to 1
- resolved_mask: int32 [64], P('grp'), may hold values from 0 to 1
- crop_positions: int32 [64], P('grp'), may hold values from 0 to 12799, as said below
- relative_position_table: bfloat16 [65, 128], replicated, may hold values from -6 to 6
- column_query_key_value_gate: bfloat16 [256, 1024], replicated, may hold values from -48 to 48
- vertical_attention_projector: bfloat16 [256, 256], replicated, may hold values from -1.5 to 1.5
- expansion_coefficients: bfloat16 [256, 1024], replicated, may hold values from -0.375 to 0.375
- contraction_coefficients: bfloat16 [1024, 256], replicated, may hold values from -0.1875 to 0.1875
- operand_duo_projector: bfloat16 [256, 64], replicated, may hold values from -0.375 to 0.375
- tensor_product_projector: bfloat16 [1024, 128], replicated, may hold values from -2 to 2
- triangle_query_key_value_gate: bfloat16 [128, 512], replicated, may hold values from -48 to 48
- triangle_bias_weight: bfloat16 [128, 4], replicated, may hold values from -0.5 to 0.5
- triangle_output_weight: bfloat16 [128, 128], replicated, may hold values from -2 to 2
- pair_up_weight: bfloat16 [128, 512], replicated, may hold values from -0.5 to 0.5
- pair_down_weight: bfloat16 [512, 128], replicated, may hold values from -0.25 to 0.25
Outputs:
- refreshed_homologs: bfloat16 [128, 64, 256], P(('grp', 'pb'), ('row', 'br'))
- pair_updated: bfloat16 [64, 64, 128], P(('grp', 'row', 'br'), 'pb')
Inputs may be any that keep to these rules, and one draw needn't show every extreme that they name: `crop_positions`: strictly increasing; the last entry is exactly 12799.
All inputs are finite; a program needn't handle non-finite values.
Results may differ from a plain program's by a relative error of at most 0.012.
Values may be sent and summed in bfloat16 or wider, within the bound.
A program may use at most 64 MiB of HBM per device.

v0:
```python
import jax
import jax.numpy as jnp
from jax import lax
from jax.sharding import PartitionSpec as P

VERTICAL_ATTENDS = 8
TRI_HEADS = 4
SUBSPACE_DEPTH = 32
RELPOS_MAX = 32


NORM_EPS = 1e-05
MASK_NEGATIVE = 1000000000.0


def layer_normalize(values):
    values = values.astype(jnp.float32)
    centre = jnp.mean(values, axis=-1, keepdims=True)
    centred = values - centre
    spread = jnp.mean(centred * centred, axis=-1, keepdims=True)
    return (centred * lax.rsqrt(spread + NORM_EPS)).astype(jnp.bfloat16)


def on_device(
    homolog_representation,
    pair_state,
    genuine_chain_indicator,
    resolved_mask,
    crop_positions,
    relative_position_table,
    column_query_key_value_gate,
    vertical_attention_projector,
    expansion_coefficients,
    contraction_coefficients,
    operand_duo_projector,
    tensor_product_projector,
    triangle_query_key_value_gate,
    triangle_bias_weight,
    triangle_output_weight,
    pair_up_weight,
    pair_down_weight,
):
    sequence_local, pair_row_slice, alignment_width = homolog_representation.shape
    pair_columns = pair_state.shape[1]
    pair_channel_width = pair_state.shape[2]
    residues = resolved_mask.shape[0]
    group_count = lax.axis_size("pb")
    group_position = lax.axis_index("pb")
    tri_local = TRI_HEADS // group_count
    score_scale = SUBSPACE_DEPTH ** (-0.5)
    outer_width = operand_duo_projector.shape[1] // 2
    standardized_representation = layer_normalize(homolog_representation)
    reshaped_standardized = standardized_representation.reshape(
        sequence_local * pair_row_slice, alignment_width
    )
    linear_mapped_representation = jnp.dot(
        reshaped_standardized, column_query_key_value_gate, preferred_element_type=jnp.float32
    ).astype(jnp.bfloat16)
    linear_mapped_representation = linear_mapped_representation.reshape(
        sequence_local, pair_row_slice, 4, VERTICAL_ATTENDS, SUBSPACE_DEPTH
    )
    query_matrix_rows = linear_mapped_representation[:, :, 0]
    key_matrix_rows = linear_mapped_representation[:, :, 1]
    value_matrix_rows = linear_mapped_representation[:, :, 2]
    gate_values_rows = linear_mapped_representation[:, :, 3]
    sequence_bias = (genuine_chain_indicator.astype(jnp.float32) - 1.0) * MASK_NEGATIVE
    starting_maximum = jnp.full(
        (pair_row_slice, VERTICAL_ATTENDS, sequence_local), -jnp.inf, jnp.float32
    )
    starting_total = jnp.zeros((pair_row_slice, VERTICAL_ATTENDS, sequence_local), jnp.float32)
    starting_sum = jnp.zeros(
        (pair_row_slice, VERTICAL_ATTENDS, sequence_local, SUBSPACE_DEPTH), jnp.float32
    )
    soft_top = starting_maximum
    soft_total = starting_total
    weighted_sum = starting_sum
    key_piece = lax.all_gather(key_matrix_rows, "pb", axis=0, tiled=True)
    value_piece = lax.all_gather(value_matrix_rows, "pb", axis=0, tiled=True)
    scores = (
        jnp.einsum(
            "schd,tchd->chst", query_matrix_rows, key_piece, preferred_element_type=jnp.float32
        )
        * score_scale
        + sequence_bias
    )
    new_top = jnp.max(scores, axis=-1)
    exp_scores = jnp.exp(scores - new_top[..., None])
    rescale = jnp.exp(soft_top - new_top)
    soft_total = soft_total * rescale + jnp.sum(exp_scores, axis=-1)
    weighted_sum = weighted_sum * rescale[..., None] + jnp.einsum(
        "chst,tchd->chsd",
        exp_scores.astype(jnp.bfloat16),
        value_piece,
        preferred_element_type=jnp.float32,
    )
    soft_top, soft_total, weighted_sum = (new_top, soft_total, weighted_sum)
    mixed_out = jnp.transpose(weighted_sum / soft_total[..., None], (2, 0, 1, 3))
    mixed_contributions = (
        (jax.nn.sigmoid(gate_values_rows.astype(jnp.float32)) * mixed_out)
        .astype(jnp.bfloat16)
        .reshape(sequence_local * pair_row_slice, alignment_width)
    )
    intermediate_representation = homolog_representation.astype(jnp.float32).reshape(
        sequence_local * pair_row_slice, alignment_width
    ) + jnp.dot(
        mixed_contributions, vertical_attention_projector, preferred_element_type=jnp.float32
    )
    expanded_activation = jax.nn.relu(
        jnp.dot(
            layer_normalize(intermediate_representation),
            expansion_coefficients,
            preferred_element_type=jnp.float32,
        )
    ).astype(jnp.bfloat16)
    refreshed_homologs = (
        (
            intermediate_representation
            + jnp.dot(
                expanded_activation, contraction_coefficients, preferred_element_type=jnp.float32
            )
        )
        .astype(jnp.bfloat16)
        .reshape(sequence_local, pair_row_slice, alignment_width)
    )
    device_local_mask = lax.dynamic_slice_in_dim(
        genuine_chain_indicator, group_position * sequence_local, sequence_local
    ).astype(jnp.float32)
    tensor_operand_entries = jnp.dot(
        reshaped_standardized, operand_duo_projector, preferred_element_type=jnp.float32
    ).reshape(sequence_local, pair_row_slice, 2 * outer_width)
    tensor_operand_entries = (tensor_operand_entries * device_local_mask[:, None, None]).astype(
        jnp.bfloat16
    )
    left_cols = tensor_operand_entries[:, :, :outer_width]
    right_cols = tensor_operand_entries[:, :, outer_width:]
    right_all = lax.all_gather(right_cols, ("row", "br"), axis=1, tiled=True)
    sequence_total = jnp.sum(genuine_chain_indicator.astype(jnp.float32))
    left_all = lax.all_gather(left_cols, "pb", axis=0, tiled=True)
    right_cells = lax.all_to_all(right_all, "pb", split_axis=1, concat_axis=0, tiled=True)
    group_total = left_all.shape[0] // sequence_local
    left_groups = left_all.reshape(group_total, sequence_local, pair_row_slice, outer_width)
    right_groups = right_cells.reshape(group_total, sequence_local, pair_columns, outer_width)

    def cell_row(row_left):
        outer_prod = jnp.einsum(
            "gsc,gsje->gjce", row_left, right_groups, preferred_element_type=jnp.float32
        ).astype(jnp.bfloat16)
        projected = jnp.dot(
            outer_prod.reshape(group_total * pair_columns, outer_width * outer_width),
            tensor_product_projector,
            preferred_element_type=jnp.float32,
        )
        return jnp.sum(
            projected.reshape(group_total, pair_columns, pair_channel_width) / sequence_total,
            axis=0,
        )

    opm_direct = lax.map(cell_row, jnp.transpose(left_groups, (2, 0, 1, 3)))
    row_first = lax.axis_index(("row", "br")) * pair_row_slice
    col_first = group_position * pair_columns
    row_places = lax.dynamic_slice_in_dim(crop_positions, row_first, pair_row_slice)
    col_places = lax.dynamic_slice_in_dim(crop_positions, col_first, pair_columns)
    rel_bins = (
        jnp.clip(row_places[:, None] - col_places[None, :], -RELPOS_MAX, RELPOS_MAX) + RELPOS_MAX
    )
    bin_count = 2 * RELPOS_MAX + 1
    one_hot = (rel_bins[:, :, None] == jnp.arange(bin_count, dtype=jnp.int32)).astype(jnp.bfloat16)
    relpos_add = jnp.dot(
        one_hot.reshape(pair_row_slice * pair_columns, bin_count),
        relative_position_table,
        preferred_element_type=jnp.float32,
    )
    pair_in = pair_state.astype(jnp.float32) + relpos_add.reshape(
        pair_row_slice, pair_columns, pair_channel_width
    )
    pair_norm = layer_normalize(pair_in).reshape(pair_row_slice * pair_columns, pair_channel_width)
    tri_proj = jnp.dot(
        pair_norm, triangle_query_key_value_gate, preferred_element_type=jnp.float32
    ).astype(jnp.bfloat16)
    tri_proj = tri_proj.reshape(pair_row_slice, pair_columns, TRI_HEADS, 4 * SUBSPACE_DEPTH)
    tri_bias = jnp.dot(pair_norm, triangle_bias_weight, preferred_element_type=jnp.float32).astype(
        jnp.bfloat16
    )
    tri_bias = tri_bias.reshape(pair_row_slice, pair_columns, TRI_HEADS)
    own_proj, own_bias = (
        lax.all_to_all(tri_proj, "pb", split_axis=2, concat_axis=1, tiled=True),
        lax.all_to_all(tri_bias, "pb", split_axis=2, concat_axis=1, tiled=True),
    )
    strips = lax.all_gather(own_bias, ("row", "br"), axis=0, tiled=True)
    key_mask = (resolved_mask.astype(jnp.float32) - 1.0) * MASK_NEGATIVE
    head_bias = jnp.transpose(strips, (2, 0, 1)).astype(jnp.float32) + key_mask

    def attend_row(row_proj):
        row_split = row_proj.reshape(residues, tri_local, 4, SUBSPACE_DEPTH)
        row_query = row_split[:, :, 0]
        row_keys = row_split[:, :, 1]
        row_values = row_split[:, :, 2]
        row_gates = row_split[:, :, 3]
        scores = (
            jnp.einsum("jhd,khd->hjk", row_query, row_keys, preferred_element_type=jnp.float32)
            * score_scale
            + head_bias
        )
        row_top = jnp.max(scores, axis=-1, keepdims=True)
        exp_scores = jnp.exp(scores - row_top)
        row_total = jnp.sum(exp_scores, axis=-1)
        row_mixed = (
            jnp.einsum(
                "hjk,khd->jhd",
                exp_scores.astype(jnp.bfloat16),
                row_values,
                preferred_element_type=jnp.float32,
            )
            / jnp.transpose(row_total)[:, :, None]
        )
        row_gated = jax.nn.sigmoid(row_gates.astype(jnp.float32)) * row_mixed
        return row_gated.astype(jnp.bfloat16).reshape(residues, tri_local * SUBSPACE_DEPTH)

    tri_out = lax.map(attend_row, own_proj)
    returned = lax.all_to_all(tri_out, "pb", split_axis=1, concat_axis=2, tiled=True)
    tri_update = jnp.dot(
        returned.reshape(pair_row_slice * pair_columns, TRI_HEADS * SUBSPACE_DEPTH),
        triangle_output_weight,
        preferred_element_type=jnp.float32,
    )
    pair_mid = (
        pair_in + tri_update.reshape(pair_row_slice, pair_columns, pair_channel_width) + opm_direct
    )
    pair_flat = pair_mid.reshape(pair_row_slice * pair_columns, pair_channel_width)
    pair_hidden = jax.nn.relu(
        jnp.dot(layer_normalize(pair_flat), pair_up_weight, preferred_element_type=jnp.float32)
    ).astype(jnp.bfloat16)
    pair_updated = (
        pair_flat + jnp.dot(pair_hidden, pair_down_weight, preferred_element_type=jnp.float32)
    ).astype(jnp.bfloat16)
    return (
        refreshed_homologs,
        pair_updated.reshape(pair_row_slice, pair_columns, pair_channel_width),
    )


def solution(mesh):
    return jax.shard_map(
        on_device,
        mesh=mesh,
        in_specs=(
            P(("grp", "pb"), ("row", "br"), None),
            P(("grp", "row", "br"), "pb", None),
            P("grp"),
            P("grp"),
            P("grp"),
            P(),
            P(),
            P(),
            P(),
            P(),
            P(),
            P(),
            P(),
            P(),
            P(),
            P(),
            P(),
        ),
        out_specs=(P(("grp", "pb"), ("row", "br"), None), P(("grp", "row", "br"), "pb", None)),
        check_vma=False,
    )
```

profile of v0, /device:TPU:0, one launch (start us, length us, event | category | flops | bytes accessed | tf_op | source)
XLA Modules:
  0.0 139.6 jit_solution(2619255453935055149)
XLA Ops:
  0.7 0.8 dynamic_slice.17
  1.4 0.7 dynamic_slice.18
  2.3 1.1 fusion.56
  3.6 0.8 convolution_convert_fusion.3
  4.5 0.7 reshape.217
  5.2 4.2 %all-to-all-start.1 = ((bf16[2,2,128]{2,1,0:T(2,128)(2,1)}), bf16[2,2,128]{2,1,0:T(2,128)(2,1)}, u32[]{:S(2)}, u32[]{:S(2)}) async-start(bf16[2,2,128]{2,1,0:T(2,128)(2,1)} %reshape.217), calls=%async_computation.1 | async-start | bytes 2048 | tf_op jit(solution)/shard_map/all_to_all | solution.py:187
  9.4 1.0 convert_reduce_fusion
  10.5 0.9 reshape.193
  11.4 1.7 %convolution_convert_fusion.2 = bf16[128,512]{1,0:T(8,128)(2,1)} fusion(bf16[128,128]{1,0:T(8,128)(2,1)S(1)} %bitcast.190, bf16[128,512]{1,0:T(8,128)(2,1)} %param.33), kind=kOutput, calls=%fused_computation.41 | convolution fusion | flops 16842752 | bytes 294912 | tf_op jit(solution)/shard_map/dot_general | solution.py:177
  13.1 1.8 %convert_reduce_fusion.1 = (f32[]{:T(128)}, f32[128]{0:T(128)}) fusion(s32[128]{0:T(128)} %param.23), kind=kLoop, calls=%fused_computation.95 | loop fusion | flops 511 | bytes 1028 | tf_op jit(solution)/shard_map/reduce_sum | solution.py:137
  14.9 0.7 dynamic-slice_convert_fusion
  15.7 1.1 multiply_reduce_fusion.1
  16.8 1.1 multiply_convert_fusion.1
  18.5 1.6 %reshape.195 = bf16[64,4,4,8,32]{4,3,2,1,0:T(8,128)(2,1)S(1)} reshape(bf16[256,1024]{1,0:T(8,128)(2,1)S(1)} %convolution_convert_fusion.1) | data formatting | bytes 1048576 | tf_op jit(solution)/shard_map/reshape | solution.py:59
  20.1 1.4 fusion.52
  21.5 15.2 %all-gather = bf16[128,4,1,8,32]{4,3,2,1,0:T(8,128)(2,1)S(1)} all-gather(bf16[64,4,1,8,32]{4,3,2,1,0:T(8,128)(2,1)S(1)} %get-tuple-element.94), channel_id=2, replica_groups=mesh['grp'=1,'row'=8,'br'=2,'pb'=2] {'pb'}, dimensions={0}, use_global_device_ids=true | all-gather | bytes 393216 | tf_op jit(solution)/shard_map/all_gather | solution.py:77
  36.7 1.1 copy.86
  38.3 1.2 fusion.54
  40.2 0.6 fusion.29
  41.4 13.8 %all-gather.1 = bf16[128,4,1,8,32]{4,3,2,1,0:T(8,128)(2,1)S(1)} all-gather(bf16[64,4,1,8,32]{4,3,2,1,0:T(8,128)(2,1)S(1)} %get-tuple-element.92), channel_id=3, replica_groups=mesh['grp'=1,'row'=8,'br'=2,'pb'=2] {'pb'}, dimensions={0}, use_global_device_ids=true | all-gather | bytes 393216 | tf_op jit(solution)/shard_map/all_gather | solution.py:78
  55.2 1.1 copy.87
  56.3 1.6 %copy.109 = bf16[64,4,1,8,32]{0,4,3,1,2:T(8,128)(2,1)S(1)} copy(bf16[64,4,1,8,32]{4,3,2,1,0:T(8,128)(2,1)} %get-tuple-element.93) | data formatting | bytes 262144
  57.9 1.2 fusion.20
  59.1 0.8 copy.88
  60.9 0.7 copy.89
  61.5 3.4 %all-to-all-start = ((bf16[4,32,4,128]{3,1,0,2:T(8,128)(2,1)}), bf16[4,32,4,128]{3,1,0,2:T(8,128)(2,1)S(1)}, u32[]{:S(2)}, u32[]{:S(2)}) async-start(bf16[4,32,4,128]{3,1,0,2:T(8,128)(2,1)} %copy.89), calls=%async_computation | async-start | bytes 262144 | tf_op jit(solution)/shard_map/all_to_all | solution.py:186
  64.9 0.8 reshape.218
  65.8 21.6 %all_gather.17 = bf16[64,64,2]{1,2,0:T(2,128)(2,1)S(1)} all-gather(bf16[4,64,2]{1,2,0:T(2,128)(2,1)S(1)} %all_to_all.55), channel_id=1, replica_groups=mesh['grp'=1,'row'=8,'br'=2,'pb'=2] {'row','br'}, dimensions={0}, use_global_device_ids=true | all-gather | bytes 17408 | tf_op jit(solution)/shard_map/all_gather | solution.py:189
  87.5 2.3 %while.20 = (s32[]{:T(128)}, bf16[4,64,64]{1,2,0:T(8,128)(2,1)S(1)}, bf16[4,64,2,128]{3,1,2,0:T(8,128)(2,1)S(1)}, f32[2,64,64]{1,2,0:T(8,128)S(1)}, s32[]{:T(128)}) while((s32[]{:T(128)}, bf16[4,64,64]{1,2,0:T(8,128)(2,1)S(1)}, bf16[4,64,2,128]{3,1,2,0:T(8,128)(2,1)S(1)}, f32[2,64,64]{1,2,0:T(8,128)S(1)}, s32[]{:T(128)}) %tuple.58), condition=%wide.region_11.12_spmd, body=%wide.region_8.11_spmd.sunk | while | flops 1134338 | bytes 437829 | solution.py:219
  89.9 0.7 reshape.219
  90.7 3.3 %all-to-all-start.2 = ((bf16[2,2,4096]{2,1,0:T(2,128)(2,1)}), bf16[2,2,4096]{2,1,0:T(2,128)(2,1)S(1)}, u32[]{:S(2)}, u32[]{:S(2)}) async-start(bf16[2,2,4096]{2,1,0:T(2,128)(2,1)} %reshape.219), calls=%async_computation.2 | async-start | bytes 65536 | tf_op jit(solution)/shard_map/all_to_all | solution.py:220
  93.9 18.9 %all_gather.19 = bf16[64,64,32]{0,2,1:T(8,128)(2,1)S(1)} all-gather(bf16[64,4,32]{0,2,1:T(8,128)(2,1)S(1)} %get-tuple-element.96), channel_id=1, replica_groups=mesh['grp'=1,'row'=8,'br'=2,'pb'=2] {'row','br'}, dimensions={1}, use_global_device_ids=true | all-gather | bytes 278528 | tf_op jit(solution)/shard_map/all_gather | solution.py:136
  112.8 1.1 reshape.215
  114.0 5.4 %all_gather.18 = bf16[128,4,32]{2,1,0:T(4,128)(2,1)S(1)} all-gather(bf16[64,4,32]{2,1,0:T(4,128)(2,1)S(1)} %copy.99), channel_id=1, replica_groups=mesh['grp'=1,'row'=8,'br'=2,'pb'=2] {'pb'}, dimensions={0}, use_global_device_ids=true | all-gather | bytes 49152 | tf_op jit(solution)/shard_map/all_gather | solution.py:138
  119.6 3.5 %all-to-all-start.3 = ((bf16[2,2,32768]{2,1,0:T(2,128)(2,1)}), bf16[2,2,32768]{2,1,0:T(2,128)(2,1)S(1)}, u32[]{:S(2)}, u32[]{:S(2)}) async-start(bf16[2,2,32768]{2,1,0:T(2,128)(2,1)} %reshape.215), calls=%async_computation.3 | async-start | bytes 524288 | tf_op jit(solution)/shard_map/all_to_all | solution.py:139
  123.0 1.6 %fusion.23 = bf16[256,256]{1,0:T(8,128)(2,1)S(1)} fusion(f32[256,256]{1,0:T(8,128)S(1)} %get-tuple-element.103, bf16[1024,256]{1,0:T(8,128)(2,1)S(1)} %copy-done.8, bf16[256,1024]{1,0:T(8,128)(2,1)} %param.29, f32[256]{0:T(256)S(1)} %add_rsqrt_fusion.3, f32[256]{0:T(256)S(1)} %broadcast_multiply_fusion.3), kind=kOutput, calls=%fused_computation.40 | convolution fusion | flops 269287424 | bytes 1443840 | tf_op jit(solution)/shard_map/dot_general | solution.py:118
  124.7 0.7 reshape.197
  125.6 2.8 %all-to-all-done.3 = bf16[2,2,32768]{2,1,0:T(2,128)(2,1)S(1)} async-done(((bf16[2,2,32768]{2,1,0:T(2,128)(2,1)}), bf16[2,2,32768]{2,1,0:T(2,128)(2,1)S(1)}, u32[]{:S(2)}, u32[]{:S(2)}) %all-to-all-start.3) | async-done | bytes 262176 | tf_op jit(solution)/shard_map/all_to_all | solution.py:139
  128.8 9.1 %while.21 = (s32[]{:T(128)}, f32[4,32,128]{2,1,0:T(8,128)S(1)}, bf16[4,2,64,32]{2,3,1,0:T(8,128)(2,1)S(1)}, bf16[2,64,32,32]{1,3,2,0:T(8,128)(2,1)S(1)}, bf16[10...) while((s32[]{:T(128)}, f32[4,32,128]{2,1,0:T(8,128)S(1)}, bf16[4,2,64,32]{2,3,1,0:T(8,128)(2,1)S(1)}, ...), condition=%wide.region_15.16_spmd, body=%wide.region_13.15_spmd.sunk | while | flops 25243648 | bytes 1376345 | solution.py:158
  128.8 0.9 fusion.92
  130.3 0.8 fusion.93
  131.1 0.9 fusion.92
  132.6 0.8 fusion.93
  133.4 0.9 fusion.92
  134.8 0.8 fusion.93
  135.7 0.9 fusion.92
  137.1 0.8 fusion.93
  138.7 0.9 fusion.28
  (101 shorter events, 10.0 us)
Async XLA Ops:
  0.6 17.6 %copy-start = (bf16[256,1024]{1,0:T(8,128)(2,1)S(1)}, bf16[256,1024]{1,0:T(8,128)(2,1)}, u32[]{:S(2)}) copy-start(bf16[256,1024]{1,0:T(8,128)(2,1)} %param.27) | copy-start | bytes 1572868
  0.6 17.3 %copy-start.9 = (bf16[256,64]{0,1:T(8,128)(2,1)S(1)}, bf16[256,64]{0,1:T(8,128)(2,1)}, u32[]{:S(2)}) copy-start(bf16[256,64]{0,1:T(8,128)(2,1)} %param.31) | copy-start | bytes 98308
  5.2 56.3 %all-to-all-start.1 = ((bf16[2,2,128]{2,1,0:T(2,128)(2,1)}), bf16[2,2,128]{2,1,0:T(2,128)(2,1)}, u32[]{:S(2)}, u32[]{:S(2)}) async-start(bf16[2,2,128]{2,1,0:T(2,128)(2,1)} %reshape.217), calls=%async_computation.1 | async-start | bytes 2048 | tf_op jit(solution)/shard_map/all_to_all | solution.py:187
  21.5 16.3 %copy-start.2 = (bf16[64,4,1,8,32]{4,3,2,1,0:T(8,128)(2,1)S(1)}, bf16[64,4,1,8,32]{4,3,2,1,0:T(8,128)(2,1)}, u32[]{:S(2)}) copy-start(bf16[64,4,1,8,32]{4,3,2,1,0:T(8,128)(2,1)} %get-tuple-element.95) | copy-start | bytes 393220
  57.9 2.4 %copy-start.6 = (bf16[256,256]{1,0:T(8,128)(2,1)S(1)}, bf16[256,256]{1,0:T(8,128)(2,1)}, u32[]{:S(2)}) copy-start(bf16[256,256]{1,0:T(8,128)(2,1)} %param.28) | copy-start | bytes 393220
  59.1 1.7 %copy-start.10 = (s32[64]{0:T(128)S(1)}, s32[64]{0:T(128)}, u32[]{:S(2)}) copy-start(s32[64]{0:T(128)} %param.24) | copy-start | bytes 772
  59.1 1.7 %copy-start.3 = (bf16[128,512]{1,0:T(8,128)(2,1)S(1)}, bf16[128,512]{1,0:T(8,128)(2,1)}, u32[]{:S(2)}) copy-start(bf16[128,512]{1,0:T(8,128)(2,1)} %convolution_convert_fusion.2) | copy-start | bytes 393220
  61.5 26.0 %all-to-all-start = ((bf16[4,32,4,128]{3,1,0,2:T(8,128)(2,1)}), bf16[4,32,4,128]{3,1,0,2:T(8,128)(2,1)S(1)}, u32[]{:S(2)}, u32[]{:S(2)}) async-start(bf16[4,32,4,128]{3,1,0,2:T(8,128)(2,1)} %copy.89), calls=%async_computation | async-start | bytes 262144 | tf_op jit(solution)/shard_map/all_to_all | solution.py:186
  89.8 33.2 %copy-start.8 = (bf16[1024,256]{1,0:T(8,128)(2,1)S(1)}, bf16[1024,256]{1,0:T(8,128)(2,1)}, u32[]{:S(2)}) copy-start(bf16[1024,256]{1,0:T(8,128)(2,1)} %param.30) | copy-start | bytes 1572868
  90.7 28.9 %all-to-all-start.2 = ((bf16[2,2,4096]{2,1,0:T(2,128)(2,1)}), bf16[2,2,4096]{2,1,0:T(2,128)(2,1)S(1)}, u32[]{:S(2)}, u32[]{:S(2)}) async-start(bf16[2,2,4096]{2,1,0:T(2,128)(2,1)} %reshape.219), calls=%async_computation.2 | async-start | bytes 65536 | tf_op jit(solution)/shard_map/all_to_all | solution.py:220
  114.0 14.8 %copy-start.1 = (bf16[1024,128]{1,0:T(8,128)(2,1)S(1)}, bf16[1024,128]{1,0:T(8,128)(2,1)}, u32[]{:S(2)}) copy-start(bf16[1024,128]{1,0:T(8,128)(2,1)} %param.32) | copy-start | bytes 786436
  119.6 8.9 %all-to-all-start.3 = ((bf16[2,2,32768]{2,1,0:T(2,128)(2,1)}), bf16[2,2,32768]{2,1,0:T(2,128)(2,1)S(1)}, u32[]{:S(2)}, u32[]{:S(2)}) async-start(bf16[2,2,32768]{2,1,0:T(2,128)(2,1)} %reshape.215), calls=%async_computation.3 | async-start | bytes 524288 | tf_op jit(solution)/shard_map/all_to_all | solution.py:139
  128.8 9.2 %copy-start.7 = (bf16[128,128]{1,0:T(8,128)(2,1)S(1)}, bf16[128,128]{1,0:T(8,128)(2,1)}, u32[]{:S(2)}) copy-start(bf16[128,128]{1,0:T(8,128)(2,1)} %param.35) | copy-start | bytes 98308
  128.8 9.9 %copy-start.4 = (bf16[512,128]{1,0:T(8,128)(2,1)S(1)}, bf16[512,128]{1,0:T(8,128)(2,1)}, u32[]{:S(2)}) copy-start(bf16[512,128]{1,0:T(8,128)(2,1)} %param.37) | copy-start | bytes 393220
  128.8 9.9 %copy-start.5 = (bf16[128,512]{1,0:T(8,128)(2,1)S(1)}, bf16[128,512]{1,0:T(8,128)(2,1)}, u32[]{:S(2)}) copy-start(bf16[128,512]{1,0:T(8,128)(2,1)} %param.36) | copy-start | bytes 393220
where the time goes:
time: 140 us
  blocking collectives  74.8 us (53%)
  local copies, waits for them, and re-layouts  19.8 us (14%)
  matrix products  17.8 us (13%)
  starting transfers between devices  14.3 us (10%)
  other arithmetic  8.7 us (6%)
  waiting for transfers between devices  2.79 us (2%)
    all_gather x1, blocking collectives, on_device(): strips = lax.all_gather(own_bias, ('row', 'br'), axis=0, tiled=True)  21.6 us
    all_gather x1, blocking collectives, on_device(): right_all = lax.all_gather(right_cols, ('row', 'br'), axis=1, tiled=True)  18.9 us
    all_gather x1, blocking collectives, on_device(): key_piece = lax.all_gather(key_matrix_rows, 'pb', axis=0, tiled=True)  15.2 us
    all_gather x1, blocking collectives, on_device(): value_piece = lax.all_gather(value_matrix_rows, 'pb', axis=0, tiled=True)  13.8 us
    unnamed x30, local copies, waits for them, and re-layouts  5.97 us
    all_gather x1, blocking collectives, on_device(): left_all = lax.all_gather(left_cols, 'pb', axis=0, tiled=True)  5.39 us
    all_to_all x1, starting transfers between devices, on_device(): lax.all_to_all(tri_bias, 'pb', split_axis=2, concat_axis=1, tiled=True)  4.21 us
    dot_general x4, matrix products, cell_row(): jnp.einsum('gsc,gsje->gjce', row_left, right_groups, preferred_element_ty...  3.51 us
  transfers between devices with their start and end apart: 4, of which 1 were waited for; matrix products, arithmetic and copies ran while one was open for 20% of the time, Pallas kernels for 0%

commit v1 on v0

v1 whole, which is shorter than its diff:
```python
import functools

import jax
import jax.numpy as jnp
from jax import lax
from jax.experimental import pallas as pl
from jax.experimental.pallas import tpu as pltpu
from jax.sharding import PartitionSpec as P

VERTICAL_ATTENDS = 8
TRI_HEADS = 4
SUBSPACE_DEPTH = 32
RELPOS_MAX = 32

NORM_EPS = 1e-05
MASK_NEGATIVE = 1000000000.0
LANES = 128
SUBLANES = 8
MESH = pl.DeviceIdType.MESH
F32 = jnp.float32
BF16 = jnp.bfloat16

WEIGHTS = (
    "rel", "qkvg", "vproj", "expand", "contract", "duo", "tensor", "tri", "tbias", "tout", "up", "down",
)


def normalize(values):
    centre = jnp.mean(values, axis=-1, keepdims=True)
    centred = values - centre
    spread = jnp.mean(centred * centred, axis=-1, keepdims=True)
    return (centred * lax.rsqrt(spread + NORM_EPS)).astype(BF16)


def matmul(a, b):
    return jnp.dot(a, b, preferred_element_type=F32)


def matmul_nt(a, b):
    return lax.dot_general(a, b, (((1,), (1,)), ((), ())), preferred_element_type=F32)


def matmul_tn(a, b):
    return lax.dot_general(a, b, (((0,), (0,)), ((), ())), preferred_element_type=F32)


def softmax_rows(scores):
    exp_scores = jnp.exp(scores - jnp.max(scores, axis=-1, keepdims=True))
    return (exp_scores / jnp.sum(exp_scores, axis=-1, keepdims=True)).astype(BF16)


def head_stack(values, heads):
    rows, width = values.shape
    lane = lax.broadcasted_iota(jnp.int32, (rows, width), 1) // SUBSPACE_DEPTH
    return jnp.concatenate(
        [jnp.where(lane == h, values, 0.0) for h in range(heads)], axis=0
    ).astype(BF16)


def head_merge(stacked, heads):
    rows, width = stacked.shape[0] // heads, stacked.shape[1]
    lane = lax.broadcasted_iota(jnp.int32, (rows, width), 1) // SUBSPACE_DEPTH
    total = jnp.zeros((rows, width), F32)
    for h in range(heads):
        total = jnp.where(lane == h, stacked[h * rows : (h + 1) * rows], total)
    return total


def kernel(sizes, *refs):
    n_pb, n_a, n_b, n_c = sizes
    x_ref, pair_ref, chain_ref, res_ref, pos_ref, pos_smem = refs[:6]
    hbm = dict(zip(WEIGHTS, refs[6:18]))
    out_msa, out_pair = refs[18:20]
    w = dict(zip(WEIGHTS, refs[20:32]))
    (xg, pg, xn_s, k_s, v_s, left_s, msg_s, gather, bias_s, pairin_s, tkv_s, wf_s, wp_s, opm_s,
     bt_s, wsem, sx, rx, sp, rp, s1, r1, s2, r2) = refs[32:]
    rows_i, seqs, width = x_ref.shape
    cells, pwidth = pair_ref.shape
    cols = cells // rows_i
    residues = res_ref.shape[1]
    n_as = n_a // n_pb
    n_src = n_as * n_b * n_c
    hpl = LANES // SUBSPACE_DEPTH
    factor = w["duo"].shape[1] // 2
    eparts = factor // SUBLANES
    seq_blocks = n_pb * eparts * seqs // LANES
    bias_blocks = -(-residues // LANES)
    factor_rows = rows_i * SUBLANES

    grp = lax.axis_index("grp")
    row = lax.axis_index("row")
    c_me = lax.axis_index("br")
    p_me = lax.axis_index("pb")
    a_me, b_me = row // n_b, row % n_b
    scale = SUBSPACE_DEPTH ** (-0.5)

    def device(a, b, c, p):
        return (grp, a * n_b + b, c, p)

    loads = {}
    for n, name in enumerate(WEIGHTS):
        loads[name] = pltpu.make_async_copy(hbm[name], w[name], wsem.at[n])
    for name in ("qkvg", "rel", "tri", "tbias", "duo", "tensor", "vproj", "expand", "contract", "tout", "up", "down"):
        loads[name].start()

    barrier = pltpu.get_barrier_semaphore()
    for d in range(1, n_pb):
        pl.semaphore_signal(barrier, inc=1, device_id=device(a_me, b_me, c_me, (p_me + d) % n_pb), device_id_type=MESH)
    for d in range(1, n_a):
        pl.semaphore_signal(barrier, inc=1, device_id=device((a_me + d) % n_a, b_me, c_me, p_me), device_id_type=MESH)
    mates = [(db, dc) for db in range(n_b) for dc in range(n_c) if (db, dc) != (0, 0)]
    for db, dc in mates:
        pl.semaphore_signal(
            barrier, inc=1, device_id=device(a_me, (b_me + db) % n_b, (c_me + dc) % n_c, p_me), device_id_type=MESH
        )
    pl.semaphore_wait(barrier, n_pb - 1 + n_a - 1 + len(mates))

    exchange = []
    for d in range(1, n_pb):
        peer = device(a_me, b_me, c_me, (p_me + d) % n_pb)
        exchange.append((
            pltpu.make_async_remote_copy(
                src_ref=pair_ref, dst_ref=pg.at[n_pb - d], send_sem=sp.at[d], recv_sem=rp.at[n_pb - d],
                device_id=peer, device_id_type=MESH),
            pltpu.make_async_remote_copy(
                src_ref=x_ref, dst_ref=xg.at[n_pb - d], send_sem=sx.at[d], recv_sem=rx.at[n_pb - d],
                device_id=peer, device_id_type=MESH),
        ))
    for copy, _ in exchange:
        copy.start()
    for _, copy in exchange:
        copy.start()

    x_own = x_ref[...].reshape(rows_i * seqs, width)
    xn_own = normalize(x_own.astype(F32))
    loads["qkvg"].wait()
    proj = matmul(xn_own, w["qkvg"][...])
    query = proj[:, :width].astype(BF16).astype(F32)
    gate = jax.nn.sigmoid(proj[:, 3 * width :].astype(BF16).astype(F32))
    xn_s[p_me] = xn_own
    k_s[p_me] = proj[:, width : 2 * width].astype(BF16)
    v_s[p_me] = proj[:, 2 * width : 3 * width].astype(BF16)

    loads["rel"].wait()
    loads["tri"].wait()
    loads["tbias"].wait()
    loads["duo"].wait()
    loads["tensor"].wait()
    tri_w = w["tri"][...].astype(F32)
    tri_w = jnp.concatenate(
        [
            tri_w[:, (h * 4 + kind) * SUBSPACE_DEPTH : (h * 4 + kind + 1) * SUBSPACE_DEPTH]
            for kind in range(4)
            for h in range(TRI_HEADS)
        ],
        axis=1,
    ).astype(BF16)
    wf_s[...] = w["tensor"][...].astype(F32)
    for e in range(factor):
        wp_s[e * factor : (e + 1) * factor, :] = wf_s[pl.ds(e, factor, stride=factor), :].astype(BF16)
    duo = w["duo"][...].astype(F32)
    left_w = jnp.concatenate([duo[:, :factor]] * eparts, axis=1).astype(BF16)
    right_w = jnp.transpose(duo)[factor:].astype(BF16)

    row_first = (row * n_c + c_me) * rows_i
    bins = 2 * RELPOS_MAX + 1

    def relpos(i, positions):
        offset = jnp.clip(pos_smem[row_first + i] - positions, -RELPOS_MAX, RELPOS_MAX) + RELPOS_MAX
        hot = lax.broadcasted_iota(jnp.int32, (bins, positions.shape[1]), 0) == offset
        return matmul_tn(jnp.where(hot, 1.0, 0.0).astype(BF16), w["rel"][...])

    relpos_all = [relpos(i, pos_ref[...]) for i in range(rows_i)]
    for i in range(rows_i):
        for p in range(n_pb):
            pairin_s[p, i * cols : (i + 1) * cols] = relpos_all[i][p * cols : (p + 1) * cols]
    for slot in range(1, n_pb):
        exchange[n_pb - slot - 1][0].wait_recv()
    for d in range(n_pb):
        p = (p_me + d) % n_pb
        held = pair_ref[...] if d == 0 else pg[d]
        total = pairin_s[p] + held.astype(F32)
        pairin_s[p] = total
        pn = normalize(total)
        tproj = matmul(pn, tri_w)
        tkv_s[p] = tproj[:, pwidth : 3 * pwidth].astype(BF16)
        bt = lax.dot_general(
            w["tbias"][...], pn, (((0,), (1,)), ((), ())), preferred_element_type=F32
        )
        bt_s[p] = bt
        if d == 0:
            tri_q = tproj[:, :pwidth].astype(BF16).astype(F32)
            tri_gate = jax.nn.sigmoid(tproj[:, 3 * pwidth :].astype(BF16).astype(F32))

    for slot in range(1, n_pb):
        exchange[n_pb - slot - 1][1].wait_recv()
    for d in range(1, n_pb):
        p = (p_me + d) % n_pb
        xn = normalize(xg[d].reshape(rows_i * seqs, width).astype(F32))
        xn_s[p] = xn
        kv = matmul(xn, w["qkvg"][:, width : 3 * width])
        k_s[p] = kv[:, :width].astype(BF16)
        v_s[p] = kv[:, width:].astype(BF16)

    a_slot = a_me - p_me * n_as
    is_source = jnp.logical_and(a_slot >= 0, a_slot < n_as)
    chain = chain_ref[...].astype(F32)

    def slot_of(a, b, c):
        return (a * n_b + b) * n_c + c

    first = [
        pltpu.make_async_remote_copy(
            src_ref=msg_s, dst_ref=gather.at[slot_of(a_slot, b_me, c_me)], send_sem=s1.at[d],
            recv_sem=r1.at[a_slot], device_id=device((a_me + d) % n_a, b_me, c_me, p_me), device_id_type=MESH)
        for d in range(1, n_a)
    ]

    @pl.when(is_source)
    def _():
        per_p = []
        for p in range(n_pb):
            rt = matmul_nt(right_w, xn_s[p])
            rt = rt * jnp.concatenate([chain[:, p * seqs : (p + 1) * seqs]] * rows_i, axis=1)
            per_p.append(rt)
        for p in range(n_pb):
            for j in range(rows_i):
                line = jnp.concatenate(
                    [
                        per_p[p][q * SUBLANES : (q + 1) * SUBLANES, j * seqs : (j + 1) * seqs]
                        for q in range(eparts)
                    ],
                    axis=1,
                )
                blocks = line.shape[1] // LANES
                for b in range(blocks):
                    bt_at = (p * blocks + b) * factor_rows + j * SUBLANES
                    opm_s[bt_at : bt_at + SUBLANES, :] = line[:, b * LANES : (b + 1) * LANES]
        base = seq_blocks * factor_rows
        for i in range(rows_i):
            line = jnp.concatenate(
                [bt_s[p][:, i * cols : (i + 1) * cols] for p in range(n_pb)], axis=1
            )
            if residues < LANES:
                line = jnp.concatenate([line, jnp.zeros((TRI_HEADS, LANES - residues), F32)], axis=1)
            for b in range(bias_blocks):
                at = base + b * rows_i * TRI_HEADS
                for h in range(TRI_HEADS):
                    opm_s[at + h * rows_i + i : at + h * rows_i + i + 1, :] = line[h : h + 1, b * LANES : (b + 1) * LANES]
        msg_s[...] = opm_s[: msg_s.shape[0], :].astype(BF16)
        for copy in first:
            copy.start()
        gather[slot_of(a_slot, b_me, c_me)] = msg_s[...]

    lane_part = lax.broadcasted_iota(jnp.int32, (seqs, LANES), 1) // factor
    for p in range(n_pb):
        left4 = matmul(xn_s[p], left_w)
        for i in range(rows_i):
            block = left4[i * seqs : (i + 1) * seqs]
            for q in range(eparts):
                left_s[(p * eparts + q) * seqs : (p * eparts + q + 1) * seqs, i * LANES : (i + 1) * LANES] = (
                    jnp.where(lane_part == q, block, 0.0).astype(BF16)
                )

    seq_bias = (chain - 1.0) * MASK_NEGATIVE
    mixed = []
    for r in range(rows_i):
        span = slice(r * seqs, (r + 1) * seqs)
        keys = jnp.concatenate([k_s[p, span, :] for p in range(n_pb)], axis=0)
        values = jnp.concatenate([v_s[p, span, :] for p in range(n_pb)], axis=0)
        scores = matmul_nt(head_stack(query[span], VERTICAL_ATTENDS), keys) * scale + seq_bias
        weighted = matmul(softmax_rows(scores), values)
        mixed.append((gate[span] * head_merge(weighted, VERTICAL_ATTENDS)).astype(BF16))

    second = []
    for a in range(n_as):
        slot = slot_of(a, b_me, c_me)

        @pl.when(a_slot != a)
        def _():
            pltpu.make_async_remote_copy(
                src_ref=msg_s, dst_ref=gather.at[slot], send_sem=s1.at[0], recv_sem=r1.at[a],
                device_id=device((a_me + 1) % n_a, b_me, c_me, p_me), device_id_type=MESH).wait_recv()

        for m, (db, dc) in enumerate(mates):
            copy = pltpu.make_async_remote_copy(
                src_ref=gather.at[slot], dst_ref=gather.at[slot], send_sem=s2.at[a * len(mates) + m],
                recv_sem=r2.at[slot],
                device_id=device(a_me, (b_me + db) % n_b, (c_me + dc) % n_c, p_me), device_id_type=MESH)
            copy.start()
            second.append(copy)

    loads["vproj"].wait()
    mid = x_own.astype(F32) + matmul(jnp.concatenate(mixed, axis=0), w["vproj"][...])
    loads["expand"].wait()
    hidden = jnp.maximum(matmul(normalize(mid), w["expand"][...]), 0.0).astype(BF16)
    loads["contract"].wait()
    fresh = mid + matmul(hidden, w["contract"][...])
    out_msa[...] = fresh.astype(BF16).reshape(out_msa.shape)

    for a in range(n_as):
        for db, dc in mates:
            slot = slot_of(a, (b_me + db) % n_b, (c_me + dc) % n_c)
            pltpu.make_async_remote_copy(
                src_ref=gather.at[slot], dst_ref=gather.at[slot], send_sem=s2.at[0], recv_sem=r2.at[slot],
                device_id=device(a_me, (b_me + db) % n_b, (c_me + dc) % n_c, p_me), device_id_type=MESH).wait_recv()

    right_all = jnp.concatenate(
        [
            jnp.concatenate(
                [gather[s, b * factor_rows : (b + 1) * factor_rows, :] for b in range(seq_blocks)], axis=1
            )
            for s in range(n_src)
        ],
        axis=0,
    )
    outer = matmul(right_all, left_s[...])
    opm_s[: rows_i * cols * SUBLANES, :] = jnp.concatenate(
        [outer[:, i * LANES : (i + 1) * LANES] for i in range(rows_i)], axis=0
    )
    lhs = jnp.concatenate(
        [opm_s[pl.ds(e, cells, stride=SUBLANES), :].astype(BF16) for e in range(SUBLANES)], axis=1
    )
    rhs = jnp.concatenate(
        [
            wp_s[(q * SUBLANES + e) * factor : (q * SUBLANES + e + 1) * factor, :]
            for e in range(SUBLANES)
            for q in range(eparts)
        ],
        axis=0,
    )
    opm = matmul(lhs, rhs) / jnp.sum(chain)

    base = seq_blocks * factor_rows
    for s in range(n_src):
        part = jnp.concatenate(
            [
                gather[s, base + b * rows_i * TRI_HEADS : base + (b + 1) * rows_i * TRI_HEADS, :]
                for b in range(bias_blocks)
            ],
            axis=1,
        ).astype(F32)
        for h in range(TRI_HEADS):
            bias_s[h * cols + s * rows_i : h * cols + (s + 1) * rows_i, :] = part[h * rows_i : (h + 1) * rows_i, :]
    bias = bias_s[:, :residues] + (res_ref[...].astype(F32) - 1.0) * MASK_NEGATIVE
    tri_mixed = []
    for i in range(rows_i):
        span = slice(i * cols, (i + 1) * cols)
        keys = jnp.concatenate([tkv_s[p, span, :pwidth] for p in range(n_pb)], axis=0)
        values = jnp.concatenate([tkv_s[p, span, pwidth:] for p in range(n_pb)], axis=0)
        scores = matmul_nt(head_stack(tri_q[span], TRI_HEADS), keys) * scale + bias
        weighted = matmul(softmax_rows(scores), values)
        tri_mixed.append((tri_gate[span] * head_merge(weighted, TRI_HEADS)).astype(BF16))
    loads["tout"].wait()
    pair_mid = pairin_s[p_me] + matmul(jnp.concatenate(tri_mixed, axis=0), w["tout"][...]) + opm
    loads["up"].wait()
    pair_hidden = jnp.maximum(matmul(normalize(pair_mid), w["up"][...]), 0.0).astype(BF16)
    loads["down"].wait()
    out_pair[...] = (pair_mid + matmul(pair_hidden, w["down"][...])).astype(BF16)

    for copies in exchange:
        for copy in copies:
            copy.wait_send()
    for copy in second:
        copy.wait_send()

    @pl.when(is_source)
    def _():
        for copy in first:
            copy.wait_send()


def on_device(sizes, x, pair, chain, resolved, positions, *weights):
    seqs, rows_i, width = x.shape
    cols, pwidth = pair.shape[1:]
    n_pb, n_a, n_b, n_c = sizes
    cells = rows_i * cols
    chains, residues = chain.shape[0], resolved.shape[0]
    n_as = n_a // n_pb
    n_src = n_as * n_b * n_c
    factor = weights[5].shape[1] // 2
    eparts = factor // SUBLANES
    factor_rows = rows_i * SUBLANES
    bias_blocks = -(-residues // LANES)
    msg_rows = n_pb * eparts * seqs // LANES * factor_rows + bias_blocks * rows_i * TRI_HEADS
    mates = n_b * n_c - 1
    vmem = pl.BlockSpec(memory_space=pltpu.VMEM)
    hbm = pl.BlockSpec(memory_space=pl.ANY)
    dma = pltpu.SemaphoreType.DMA
    x_t = jnp.transpose(x, (1, 0, 2))
    msa, pair_out = pl.pallas_call(
        functools.partial(kernel, sizes),
        out_shape=(
            jax.ShapeDtypeStruct((rows_i, seqs, width), BF16),
            jax.ShapeDtypeStruct((cells, pwidth), BF16),
        ),
        in_specs=[vmem] * 5 + [pl.BlockSpec(memory_space=pltpu.SMEM)] + [hbm] * len(weights),
        out_specs=(vmem, vmem),
        scratch_shapes=[pltpu.VMEM(v.shape, v.dtype) for v in weights]
        + [
            pltpu.VMEM((n_pb, rows_i, seqs, width), BF16),
            pltpu.VMEM((n_pb, cells, pwidth), BF16),
            pltpu.VMEM((n_pb, rows_i * seqs, width), BF16),
            pltpu.VMEM((n_pb, rows_i * seqs, width), BF16),
            pltpu.VMEM((n_pb, rows_i * seqs, width), BF16),
            pltpu.VMEM((n_pb * eparts * seqs, rows_i * LANES), BF16),
            pltpu.VMEM((msg_rows, LANES), BF16),
            pltpu.VMEM((n_src, msg_rows, LANES), BF16),
            pltpu.VMEM((TRI_HEADS * cols, bias_blocks * LANES), F32),
            pltpu.VMEM((n_pb, cells, pwidth), F32),
            pltpu.VMEM((n_pb, cells, 2 * pwidth), BF16),
            pltpu.VMEM(weights[6].shape, F32),
            pltpu.VMEM(weights[6].shape, BF16),
            pltpu.VMEM((max(cells * SUBLANES, msg_rows), LANES), F32),
            pltpu.VMEM((n_pb, TRI_HEADS, cells), F32),
            dma((len(weights),)),
            dma((n_pb,)),
            dma((n_pb,)),
            dma((n_pb,)),
            dma((n_pb,)),
            dma((n_a,)),
            dma((n_as,)),
            dma((n_as * mates,)),
            dma((n_src,)),
        ],
        compiler_params=pltpu.CompilerParams(
            collective_id=0, has_side_effects=True, vmem_limit_bytes=40 * 1024 * 1024
        ),
    )(
        x_t,
        pair.reshape(cells, pwidth),
        chain.reshape(1, chains),
        resolved.reshape(1, residues),
        positions.reshape(1, residues),
        positions,
        *weights,
    )
    return jnp.transpose(msa, (1, 0, 2)), pair_out.reshape(rows_i, cols, pwidth)


def solution(mesh):
    n_row, n_br, n_pb = mesh.shape["row"], mesh.shape["br"], mesh.shape["pb"]
    n_b = 2 if n_row % (2 * n_pb) == 0 else 1
    sizes = (n_pb, n_row // n_b, n_b, n_br)
    return jax.shard_map(
        functools.partial(on_device, sizes),
        mesh=mesh,
        in_specs=(
            P(("grp", "pb"), ("row", "br"), None),
            P(("grp", "row", "br"), "pb", None),
            P("grp"),
            P("grp"),
            P("grp"),
        )
        + (P(),) * 12,
        out_specs=(P(("grp", "pb"), ("row", "br"), None), P(("grp", "row", "br"), "pb", None)),
        check_vma=False,
    )
```

time: 140 us -> 34.9 us (0.25)
  the two profiles are of different devices: /device:TPU:0 before, /device:TPU:25 now
where the time goes in v1:
time: 34.9 us; the launch traced here: 34.3 us
  Pallas kernels  20.8 us (60%)
  local copies, waits for them, and re-layouts  12.8 us (37%)
  between operations  0.71 us (2%)
    pallas_call x1, Pallas kernels, on_device(): pl.pallas_call(functools.partial(kernel, sizes), out_shape=(jax.ShapeDtyp...  20.8 us
    unnamed x33, local copies, waits for them, and re-layouts  12.8 us

profile of v1, /device:TPU:25, one launch (start us, length us, event | category | flops | bytes accessed | tf_op | source)
XLA Modules:
  0.0 34.3 jit_solution(4165684048818884088)
XLA Ops:
  0.6 0.0 copy-start.3
  0.6 0.8 %copy.21.refs_14_ = bf16[128,4]{1,0:T(8,128)(2,1)S(1)} copy(bf16[128,4]{0,1:T(4,128)(2,1)} %param.30) | data formatting | bytes 2048 | tf_op args[13]
  1.5 0.9 %copy.20.refs_11_ = bf16[256,64]{1,0:T(8,128)(2,1)S(1)} copy(bf16[256,64]{0,1:T(8,128)(2,1)} %param.27) | data formatting | bytes 65536 | tf_op args[10]
  2.4 0.0 copy-start.4
  2.4 1.0 %copy.24 = bf16[64,4,256]{2,0,1:T(8,128)(2,1)S(1)} copy(bf16[64,4,256]{2,1,0:T(4,128)(2,1)} %param.17) | data formatting | bytes 262144 | tf_op args[0]
  3.3 0.0 copy-start.11
  3.3 0.0 copy-start.12
  3.4 0.0 copy-start.13
  3.4 0.0 copy-done.3
  3.4 0.0 copy-done.4
  3.4 0.6 %copy-done.11 = s32[64]{0:T(128)S(1)} copy-done((s32[64]{0:T(128)S(1)}, s32[64]{0:T(128)}, u32[]{:S(2)}) %copy-start.11) | copy-done | bytes 280
  4.0 0.0 copy-done.12
  4.0 0.0 copy-done.13
  4.0 0.0 copy-start
  4.0 1.0 %copy-done = bf16[256,1024]{1,0:T(8,128)(2,1)S(1)} copy-done((bf16[256,1024]{1,0:T(8,128)(2,1)S(1)}, bf16[256,1024]{1,0:T(8,128)(2,1)}, u32[]{:S(2)}) %copy-start) | copy-done | bytes 524312
  5.1 0.0 copy-start.1
  5.1 1.0 %copy-done.1 = bf16[256,1024]{1,0:T(8,128)(2,1)S(1)} copy-done((bf16[256,1024]{1,0:T(8,128)(2,1)S(1)}, bf16[256,1024]{1,0:T(8,128)(2,1)}, u32[]{:S(2)}) %copy-start.1) | copy-done | bytes 524312
  6.1 0.0 copy-start.2
  6.1 1.0 %copy-done.2 = bf16[1024,256]{1,0:T(8,128)(2,1)S(1)} copy-done((bf16[1024,256]{1,0:T(8,128)(2,1)S(1)}, bf16[1024,256]{1,0:T(8,128)(2,1)}, u32[]{:S(2)}) %copy-start.2) | copy-done | bytes 524312
  7.2 0.0 copy-start.5
  7.2 0.9 %copy-done.5 = bf16[128,512]{1,0:T(8,128)(2,1)S(1)} copy-done((bf16[128,512]{1,0:T(8,128)(2,1)S(1)}, bf16[128,512]{1,0:T(8,128)(2,1)}, u32[]{:S(2)}) %copy-start.5) | copy-done | bytes 131096
  8.1 0.0 copy-start.6
  8.1 0.9 %copy-done.6 = bf16[128,512]{1,0:T(8,128)(2,1)S(1)} copy-done((bf16[128,512]{1,0:T(8,128)(2,1)S(1)}, bf16[128,512]{1,0:T(8,128)(2,1)}, u32[]{:S(2)}) %copy-start.6) | copy-done | bytes 131096
  9.0 0.0 copy-start.7
  9.0 0.9 %copy-done.7 = bf16[512,128]{1,0:T(8,128)(2,1)S(1)} copy-done((bf16[512,128]{1,0:T(8,128)(2,1)S(1)}, bf16[512,128]{1,0:T(8,128)(2,1)}, u32[]{:S(2)}) %copy-start.7) | copy-done | bytes 131096
  9.9 0.0 copy-start.8
  9.9 0.8 %copy-done.8 = bf16[4,32,128]{2,1,0:T(8,128)(2,1)S(1)} copy-done((bf16[4,32,128]{2,1,0:T(8,128)(2,1)S(1)}, bf16[4,32,128]{2,1,0:T(8,128)(2,1)}, u32[]{:S(2)}) %copy-start.8) | copy-done | bytes 32792
  10.6 0.0 copy-start.9
  10.6 0.8 %copy-done.9 = bf16[128,128]{1,0:T(8,128)(2,1)S(1)} copy-done((bf16[128,128]{1,0:T(8,128)(2,1)S(1)}, bf16[128,128]{1,0:T(8,128)(2,1)}, u32[]{:S(2)}) %copy-start.9) | copy-done | bytes 32792
  11.4 0.0 copy-start.10
  11.4 0.7 %copy-done.10 = bf16[65,128]{1,0:T(8,128)(2,1)S(1)} copy-done((bf16[65,128]{1,0:T(8,128)(2,1)S(1)}, bf16[65,128]{1,0:T(8,128)(2,1)}, u32[]{:S(2)}) %copy-start.10) | copy-done | bytes 16664
  12.1 20.8 %shard_map.176 = (bf16[4,64,256]{2,1,0:T(8,128)(2,1)S(1)}, bf16[128,128]{1,0:T(8,128)(2,1)S(1)}) custom-call(bf16[4,64,256]{2,1,0:T(8,128)(2,1)S(1)} %bitcast.9, bf16[128,128]{1,0:T(8,128)(2,1)S(1)} %bitcast.12, s32[1,128]{1,0:T(1,128)S(1)} %bitcast.14, s32[1,64]{1,0:T(1,128)S(1)} %bitcast.15, s32[1,64]{1,0:T(1,128)S(1)} %bitcast.13, s32[64]{0:T(128)S(1)} %copy-done.11, ...), custom_call_target="tpu_custom_call" | custom-call | tf_op jit(solution)/shard_map/pallas_call | solution.py:391
  32.9 0.8 %copy.22 = bf16[64,4,256]{2,1,0:T(4,128)(2,1)} copy(bf16[64,4,256]{2,0,1:T(8,128)(2,1)S(1)} %bitcast.10) | data formatting | bytes 262144
  33.7 0.6 %copy.26 = bf16[4,32,128]{2,1,0:T(8,128)(2,1)} copy(bf16[4,32,128]{2,1,0:T(8,128)(2,1)S(1)} %bitcast.11) | data formatting | bytes 65536
Async XLA Ops:
  0.6 2.7 %copy-start.3 = (bf16[1024,128]{1,0:T(8,128)(2,1)S(1)}, bf16[1024,128]{1,0:T(8,128)(2,1)}, u32[]{:S(2)}) copy-start(bf16[1024,128]{1,0:T(8,128)(2,1)} %refs_12_.1) | copy-start | bytes 786436
  2.4 1.0 %copy-start.4 = (bf16[256,256]{1,0:T(8,128)(2,1)S(1)}, bf16[256,256]{1,0:T(8,128)(2,1)}, u32[]{:S(2)}) copy-start(bf16[256,256]{1,0:T(8,128)(2,1)} %refs_8_.1) | copy-start | bytes 393220
  3.3 0.7 %copy-start.11 = (s32[64]{0:T(128)S(1)}, s32[64]{0:T(128)}, u32[]{:S(2)}) copy-start(s32[64]{0:T(128)} %refs_5_.1) | copy-start | bytes 772
  3.3 0.7 %copy-start.12 = (s32[128]{0:T(128)S(1)}, s32[128]{0:T(128)}, u32[]{:S(2)}) copy-start(s32[128]{0:T(128)} %param.19) | copy-start | bytes 1540
  3.4 0.7 %copy-start.13 = (s32[64]{0:T(128)S(1)}, s32[64]{0:T(128)}, u32[]{:S(2)}) copy-start(s32[64]{0:T(128)} %param.20) | copy-start | bytes 772
  4.0 1.0 %copy-start = (bf16[256,1024]{1,0:T(8,128)(2,1)S(1)}, bf16[256,1024]{1,0:T(8,128)(2,1)}, u32[]{:S(2)}) copy-start(bf16[256,1024]{1,0:T(8,128)(2,1)} %refs_7_.1) | copy-start | bytes 1572868
  5.1 1.0 %copy-start.1 = (bf16[256,1024]{1,0:T(8,128)(2,1)S(1)}, bf16[256,1024]{1,0:T(8,128)(2,1)}, u32[]{:S(2)}) copy-start(bf16[256,1024]{1,0:T(8,128)(2,1)} %refs_9_.1) | copy-start | bytes 1572868
  6.1 1.0 %copy-start.2 = (bf16[1024,256]{1,0:T(8,128)(2,1)S(1)}, bf16[1024,256]{1,0:T(8,128)(2,1)}, u32[]{:S(2)}) copy-start(bf16[1024,256]{1,0:T(8,128)(2,1)} %refs_10_.1) | copy-start | bytes 1572868
  7.2 0.9 %copy-start.5 = (bf16[128,512]{1,0:T(8,128)(2,1)S(1)}, bf16[128,512]{1,0:T(8,128)(2,1)}, u32[]{:S(2)}) copy-start(bf16[128,512]{1,0:T(8,128)(2,1)} %refs_13_.1) | copy-start | bytes 393220
  8.1 0.9 %copy-start.6 = (bf16[128,512]{1,0:T(8,128)(2,1)S(1)}, bf16[128,512]{1,0:T(8,128)(2,1)}, u32[]{:S(2)}) copy-start(bf16[128,512]{1,0:T(8,128)(2,1)} %refs_16_.1) | copy-start | bytes 393220
  9.0 0.9 %copy-start.7 = (bf16[512,128]{1,0:T(8,128)(2,1)S(1)}, bf16[512,128]{1,0:T(8,128)(2,1)}, u32[]{:S(2)}) copy-start(bf16[512,128]{1,0:T(8,128)(2,1)} %refs_17_.1) | copy-start | bytes 393220
  9.9 0.8 %copy-start.8 = (bf16[4,32,128]{2,1,0:T(8,128)(2,1)S(1)}, bf16[4,32,128]{2,1,0:T(8,128)(2,1)}, u32[]{:S(2)}) copy-start(bf16[4,32,128]{2,1,0:T(8,128)(2,1)} %param.18) | copy-start | bytes 98308
  10.6 0.8 %copy-start.9 = (bf16[128,128]{1,0:T(8,128)(2,1)S(1)}, bf16[128,128]{1,0:T(8,128)(2,1)}, u32[]{:S(2)}) copy-start(bf16[128,128]{1,0:T(8,128)(2,1)} %refs_15_.1) | copy-start | bytes 98308
  11.4 0.7 %copy-start.10 = (bf16[65,128]{1,0:T(8,128)(2,1)S(1)}, bf16[65,128]{1,0:T(8,128)(2,1)}, u32[]{:S(2)}) copy-start(bf16[65,128]{1,0:T(8,128)(2,1)} %refs_6_.1) | copy-start | bytes 49924

commit v2 on v1

v2 whole, which is shorter than its diff:
```python
import functools

import jax
import jax.numpy as jnp
from jax import lax
from jax.experimental import pallas as pl
from jax.experimental.pallas import tpu as pltpu
from jax.sharding import PartitionSpec as P

VERTICAL_ATTENDS = 8
TRI_HEADS = 4
SUBSPACE_DEPTH = 32
RELPOS_MAX = 32

NORM_EPS = 1e-05
MASK_NEGATIVE = 1000000000.0
LANES = 128
SUBLANES = 8
MESH = pl.DeviceIdType.MESH
F32 = jnp.float32
BF16 = jnp.bfloat16

WEIGHTS = (
    "rel", "qkvg", "vproj", "expand", "contract", "duo", "tensor", "tri", "tbias", "tout", "up", "down",
)


INPUTS = (
    "chain", "duo", "positions", "scalars", "rel", "pair", "tbias", "qkvg", "tri", "tensor",
    "vproj", "expand", "contract", "resolved", "tout", "up", "down",
)


def normalize(values):
    centre = jnp.mean(values, axis=-1, keepdims=True)
    centred = values - centre
    spread = jnp.mean(centred * centred, axis=-1, keepdims=True)
    return (centred * lax.rsqrt(spread + NORM_EPS)).astype(BF16)


def matmul(a, b):
    return jnp.dot(a, b, preferred_element_type=F32)


def matmul_nt(a, b):
    return lax.dot_general(a, b, (((1,), (1,)), ((), ())), preferred_element_type=F32)


def matmul_tn(a, b):
    return lax.dot_general(a, b, (((0,), (0,)), ((), ())), preferred_element_type=F32)


def softmax_rows(scores):
    exp_scores = jnp.exp(scores - jnp.max(scores, axis=-1, keepdims=True))
    return (exp_scores * (1.0 / jnp.sum(exp_scores, axis=-1, keepdims=True))).astype(BF16)


def head_stack(values, heads):
    rows, width = values.shape
    lane = lax.broadcasted_iota(jnp.int32, (rows, width), 1) // SUBSPACE_DEPTH
    return jnp.concatenate(
        [jnp.where(lane == h, values, 0.0) for h in range(heads)], axis=0
    ).astype(BF16)


def head_merge(stacked, heads):
    rows, width = stacked.shape[0] // heads, stacked.shape[1]
    lane = lax.broadcasted_iota(jnp.int32, (rows, width), 1) // SUBSPACE_DEPTH
    total = jnp.zeros((rows, width), F32)
    for h in range(heads):
        total = jnp.where(lane == h, stacked[h * rows : (h + 1) * rows], total)
    return total


def kernel(sizes, *refs):
    n_pb, n_a, n_b, n_c = sizes
    x_ref = refs[0]
    hbm = dict(zip(INPUTS, refs[1 : 1 + len(INPUTS)]))
    out_msa, out_pair = refs[1 + len(INPUTS) : 3 + len(INPUTS)]
    w = dict(zip(INPUTS, refs[3 + len(INPUTS) : 3 + 2 * len(INPUTS)]))
    (xg, pg, xn_s, k_s, v_s, left_s, msg_s, gather, bias_s, pairin_s, tkv_s, wf_s, wp_s, opm_s,
     wsem, sx, rx, sp, rp, s1, r1, s2, r2) = refs[3 + 2 * len(INPUTS) :]
    pair_ref = w["pair"]
    rows_i, seqs, width = x_ref.shape
    cells, pwidth = pair_ref.shape
    cols = cells // rows_i
    residues = w["resolved"].shape[1]
    n_as = n_a // n_pb
    n_src = n_as * n_b * n_c
    factor = w["duo"].shape[0] // 2
    eparts = factor // SUBLANES
    seq_blocks = eparts * seqs // LANES
    factor_rows = rows_i * SUBLANES
    base = seq_blocks * factor_rows

    grp = lax.axis_index("grp")
    row = lax.axis_index("row")
    c_me = lax.axis_index("br")
    p_me = lax.axis_index("pb")
    a_me, b_me = row // n_b, row % n_b
    scale = SUBSPACE_DEPTH ** (-0.5)

    def device(a, b, c, p):
        return (grp, a * n_b + b, c, p)

    loads = {}
    for n, name in enumerate(INPUTS):
        loads[name] = pltpu.make_async_copy(hbm[name], w[name], wsem.at[n])
    for name in INPUTS:
        loads[name].start()

    barrier = pltpu.get_barrier_semaphore()
    line = [(da, dp) for da in range(n_a) for dp in range(n_pb) if (da, dp) != (0, 0)]
    mates = [(db, dc) for db in range(n_b) for dc in range(n_c) if (db, dc) != (0, 0)]
    for da, dp in line:
        pl.semaphore_signal(
            barrier, inc=1, device_id=device((a_me + da) % n_a, b_me, c_me, (p_me + dp) % n_pb), device_id_type=MESH
        )
    for db, dc in mates:
        pl.semaphore_signal(
            barrier, inc=1, device_id=device(a_me, (b_me + db) % n_b, (c_me + dc) % n_c, p_me), device_id_type=MESH
        )

    x_own = x_ref[...].reshape(rows_i * seqs, width)
    xn_own = normalize(x_own.astype(F32))
    xn_s[p_me] = xn_own
    loads["chain"].wait()
    loads["duo"].wait()
    chain = w["chain"][...].astype(F32)
    own_chain = jnp.zeros((1, seqs), F32)
    for p in range(n_pb):
        own_chain = jnp.where(p_me == p, chain[:, p * seqs : (p + 1) * seqs], own_chain)
    rt = matmul_nt(w["duo"][factor:, :], xn_own) * jnp.concatenate([own_chain] * rows_i, axis=1)
    for j in range(rows_i):
        parts = jnp.concatenate(
            [rt[q * SUBLANES : (q + 1) * SUBLANES, j * seqs : (j + 1) * seqs] for q in range(eparts)], axis=1
        )
        for b in range(seq_blocks):
            at = b * factor_rows + j * SUBLANES
            opm_s[at : at + SUBLANES, :] = parts[:, b * LANES : (b + 1) * LANES]

    row_first = (row * n_c + c_me) * rows_i
    bins = 2 * RELPOS_MAX + 1
    loads["positions"].wait()
    loads["scalars"].wait()
    loads["rel"].wait()
    for i in range(rows_i):
        offset = jnp.clip(w["scalars"][row_first + i] - w["positions"][...], -RELPOS_MAX, RELPOS_MAX) + RELPOS_MAX
        hot = lax.broadcasted_iota(jnp.int32, (bins, residues), 0) == offset
        added = matmul_tn(jnp.where(hot, 1.0, 0.0).astype(BF16), w["rel"][...])
        for p in range(n_pb):
            pairin_s[p, i * cols : (i + 1) * cols] = added[p * cols : (p + 1) * cols]
    loads["pair"].wait()
    pair_in = pairin_s[p_me] + pair_ref[...].astype(F32)
    pn_own = normalize(pair_in)
    loads["tbias"].wait()
    bt = matmul_nt(w["tbias"][...], pn_own)
    for i in range(rows_i):
        for h in range(TRI_HEADS):
            at = base + h * rows_i + i
            opm_s[at : at + 1, :cols] = bt[h : h + 1, i * cols : (i + 1) * cols]
    msg_s[...] = opm_s[: msg_s.shape[0], :].astype(BF16)

    pl.semaphore_wait(barrier, len(line) + len(mates))

    p_to, a_slot = a_me // n_as, a_me % n_as
    stays = p_to == p_me

    def slot_of(a, b, c):
        return (a * n_b + b) * n_c + c

    def first(d):
        return pltpu.make_async_remote_copy(
            src_ref=msg_s, dst_ref=gather.at[slot_of(a_slot, b_me, c_me), p_me], send_sem=s1.at[d],
            recv_sem=r1.at[a_slot * n_pb + p_me], device_id=device((a_me + d) % n_a, b_me, c_me, p_to),
            device_id_type=MESH)

    for d in range(1, n_a):
        first(d).start()

    @pl.when(jnp.logical_not(stays))
    def _():
        first(0).start()

    @pl.when(stays)
    def _():
        gather[slot_of(a_slot, b_me, c_me), p_me] = msg_s[...]

    exchange = []
    for d in range(1, n_pb):
        peer = device(a_me, b_me, c_me, (p_me + d) % n_pb)
        exchange.append((
            pltpu.make_async_remote_copy(
                src_ref=pair_ref, dst_ref=pg.at[n_pb - d], send_sem=sp.at[d], recv_sem=rp.at[n_pb - d],
                device_id=peer, device_id_type=MESH),
            pltpu.make_async_remote_copy(
                src_ref=x_ref, dst_ref=xg.at[n_pb - d], send_sem=sx.at[d], recv_sem=rx.at[n_pb - d],
                device_id=peer, device_id_type=MESH),
        ))
    for copy, _ in exchange:
        copy.start()
    for _, copy in exchange:
        copy.start()

    loads["qkvg"].wait()
    proj = matmul(xn_own, w["qkvg"][...])
    query = proj[:, :width].astype(BF16).astype(F32)
    gate = jax.nn.sigmoid(proj[:, 3 * width :].astype(BF16).astype(F32))
    k_s[p_me] = proj[:, width : 2 * width].astype(BF16)
    v_s[p_me] = proj[:, 2 * width : 3 * width].astype(BF16)

    loads["tri"].wait()
    tri_w = w["tri"][...].astype(F32)
    tri_w = jnp.concatenate(
        [
            tri_w[:, (h * 4 + kind) * SUBSPACE_DEPTH : (h * 4 + kind + 1) * SUBSPACE_DEPTH]
            for kind in range(4)
            for h in range(TRI_HEADS)
        ],
        axis=1,
    ).astype(BF16)
    tproj = matmul(pn_own, tri_w)
    tkv_s[p_me] = tproj[:, pwidth : 3 * pwidth].astype(BF16)
    tri_q = tproj[:, :pwidth].astype(BF16).astype(F32)
    tri_gate = jax.nn.sigmoid(tproj[:, 3 * pwidth :].astype(BF16).astype(F32))
    loads["tensor"].wait()
    wf_s[...] = w["tensor"][...].astype(F32)
    for e in range(SUBLANES):
        for q in range(eparts):
            at = (e * eparts + q) * factor
            wp_s[at : at + factor, :] = wf_s[pl.ds(q * SUBLANES + e, factor, stride=factor), :].astype(BF16)

    for slot in range(1, n_pb):
        exchange[n_pb - slot - 1][0].wait_recv()
    for d in range(1, n_pb):
        p = (p_me + d) % n_pb
        pn = normalize(pairin_s[p] + pg[d].astype(F32))
        tkv_s[p] = matmul(pn, tri_w[:, pwidth : 3 * pwidth]).astype(BF16)

    second = []
    for a in range(n_as):
        slot = slot_of(a, b_me, c_me)
        for p in range(n_pb):
            here = jnp.logical_and(stays, jnp.logical_and(a_slot == a, p_me == p))

            @pl.when(jnp.logical_not(here))
            def _():
                pltpu.make_async_remote_copy(
                    src_ref=msg_s, dst_ref=gather.at[slot, p], send_sem=s1.at[0], recv_sem=r1.at[a * n_pb + p],
                    device_id=device((a_me + 1) % n_a, b_me, c_me, p_me), device_id_type=MESH).wait_recv()

        for m, (db, dc) in enumerate(mates):
            copy = pltpu.make_async_remote_copy(
                src_ref=gather.at[slot], dst_ref=gather.at[slot], send_sem=s2.at[a * len(mates) + m],
                recv_sem=r2.at[slot],
                device_id=device(a_me, (b_me + db) % n_b, (c_me + dc) % n_c, p_me), device_id_type=MESH)
            copy.start()
            second.append(copy)

    for slot in range(1, n_pb):
        exchange[n_pb - slot - 1][1].wait_recv()
    for d in range(1, n_pb):
        p = (p_me + d) % n_pb
        xn = normalize(xg[d].reshape(rows_i * seqs, width).astype(F32))
        xn_s[p] = xn
        kv = matmul(xn, w["qkvg"][:, width : 3 * width])
        k_s[p] = kv[:, :width].astype(BF16)
        v_s[p] = kv[:, width:].astype(BF16)

    left_w = jnp.concatenate([w["duo"][:factor, :]] * eparts, axis=0)
    lane_part = lax.broadcasted_iota(jnp.int32, (seqs, LANES), 1) // factor
    for p in range(n_pb):
        left4 = matmul_nt(xn_s[p], left_w)
        for i in range(rows_i):
            block = left4[i * seqs : (i + 1) * seqs]
            for q in range(eparts):
                left_s[(p * eparts + q) * seqs : (p * eparts + q + 1) * seqs, i * LANES : (i + 1) * LANES] = (
                    jnp.where(lane_part == q, block, 0.0).astype(BF16)
                )

    seq_bias = (chain - 1.0) * MASK_NEGATIVE
    mixed = []
    for r in range(rows_i):
        span = slice(r * seqs, (r + 1) * seqs)
        keys = jnp.concatenate([k_s[p, span, :] for p in range(n_pb)], axis=0)
        values = jnp.concatenate([v_s[p, span, :] for p in range(n_pb)], axis=0)
        scores = matmul_nt(head_stack(query[span], VERTICAL_ATTENDS), keys) * scale + seq_bias
        weighted = matmul(softmax_rows(scores), values)
        mixed.append((gate[span] * head_merge(weighted, VERTICAL_ATTENDS)).astype(BF16))

    loads["vproj"].wait()
    mid = x_own.astype(F32) + matmul(jnp.concatenate(mixed, axis=0), w["vproj"][...])
    loads["expand"].wait()
    hidden = jnp.maximum(matmul(normalize(mid), w["expand"][...]), 0.0).astype(BF16)
    loads["contract"].wait()
    fresh = mid + matmul(hidden, w["contract"][...])
    out_msa[...] = fresh.astype(BF16).reshape(out_msa.shape)

    for a in range(n_as):
        for db, dc in mates:
            slot = slot_of(a, (b_me + db) % n_b, (c_me + dc) % n_c)
            pltpu.make_async_remote_copy(
                src_ref=gather.at[slot], dst_ref=gather.at[slot], send_sem=s2.at[0], recv_sem=r2.at[slot],
                device_id=device(a_me, (b_me + db) % n_b, (c_me + dc) % n_c, p_me), device_id_type=MESH).wait_recv()

    right_all = jnp.concatenate(
        [
            jnp.concatenate(
                [
                    gather[s, p, b * factor_rows : (b + 1) * factor_rows, :]
                    for p in range(n_pb)
                    for b in range(seq_blocks)
                ],
                axis=1,
            )
            for s in range(n_src)
        ],
        axis=0,
    )
    outer = matmul(right_all, left_s[...])
    opm_s[: cells * SUBLANES, :] = jnp.concatenate(
        [outer[:, i * LANES : (i + 1) * LANES] for i in range(rows_i)], axis=0
    )
    lhs = jnp.concatenate(
        [opm_s[pl.ds(e, cells, stride=SUBLANES), :].astype(BF16) for e in range(SUBLANES)], axis=1
    )
    opm = matmul(lhs, wp_s[...]) / jnp.sum(chain)

    for s in range(n_src):
        part = jnp.concatenate(
            [gather[s, p, base : base + rows_i * TRI_HEADS, :].astype(F32)[:, :cols] for p in range(n_pb)], axis=1
        )
        for h in range(TRI_HEADS):
            bias_s[h * cols + s * rows_i : h * cols + (s + 1) * rows_i, :] = part[h * rows_i : (h + 1) * rows_i, :]
    loads["resolved"].wait()
    bias = bias_s[...] + (w["resolved"][...].astype(F32) - 1.0) * MASK_NEGATIVE
    tri_mixed = []
    for i in range(rows_i):
        span = slice(i * cols, (i + 1) * cols)
        keys = jnp.concatenate([tkv_s[p, span, :pwidth] for p in range(n_pb)], axis=0)
        values = jnp.concatenate([tkv_s[p, span, pwidth:] for p in range(n_pb)], axis=0)
        scores = matmul_nt(head_stack(tri_q[span], TRI_HEADS), keys) * scale + bias
        weighted = matmul(softmax_rows(scores), values)
        tri_mixed.append((tri_gate[span] * head_merge(weighted, TRI_HEADS)).astype(BF16))
    loads["tout"].wait()
    pair_mid = pair_in + matmul(jnp.concatenate(tri_mixed, axis=0), w["tout"][...]) + opm
    loads["up"].wait()
    pair_hidden = jnp.maximum(matmul(normalize(pair_mid), w["up"][...]), 0.0).astype(BF16)
    loads["down"].wait()
    out_pair[...] = (pair_mid + matmul(pair_hidden, w["down"][...])).astype(BF16)

    for copies in exchange:
        for copy in copies:
            copy.wait_send()
    for copy in second:
        copy.wait_send()
    for d in range(1, n_a):
        first(d).wait_send()

    @pl.when(jnp.logical_not(stays))
    def _():
        first(0).wait_send()


def on_device(sizes, x, pair, chain, resolved, positions, *weights):
    seqs, rows_i, width = x.shape
    cols, pwidth = pair.shape[1:]
    n_pb, n_a, n_b, n_c = sizes
    cells = rows_i * cols
    chains, residues = chain.shape[0], resolved.shape[0]
    n_as = n_a // n_pb
    n_src = n_as * n_b * n_c
    arrays = dict(zip(WEIGHTS, weights))
    arrays["duo"] = arrays["duo"].T
    arrays["tbias"] = arrays["tbias"].T
    arrays["pair"] = pair.reshape(cells, pwidth)
    arrays["chain"] = chain.reshape(1, chains)
    arrays["resolved"] = resolved.reshape(1, residues)
    arrays["positions"] = positions.reshape(1, residues)
    arrays["scalars"] = positions
    inputs = [arrays[name] for name in INPUTS]
    factor = arrays["duo"].shape[0] // 2
    eparts = factor // SUBLANES
    msg_rows = eparts * seqs // LANES * rows_i * SUBLANES + rows_i * TRI_HEADS
    mates = n_b * n_c - 1
    vmem = pl.BlockSpec(memory_space=pltpu.VMEM)
    dma = pltpu.SemaphoreType.DMA
    x_t = jnp.transpose(x, (1, 0, 2))
    msa, pair_out = pl.pallas_call(
        functools.partial(kernel, sizes),
        out_shape=(
            jax.ShapeDtypeStruct((rows_i, seqs, width), BF16),
            jax.ShapeDtypeStruct((cells, pwidth), BF16),
        ),
        in_specs=[vmem] + [pl.BlockSpec(memory_space=pltpu.HBM)] * len(inputs),
        out_specs=(vmem, vmem),
        scratch_shapes=[
            (pltpu.SMEM if name == "scalars" else pltpu.VMEM)(v.shape, v.dtype) for name, v in zip(INPUTS, inputs)
        ]
        + [
            pltpu.VMEM((n_pb, rows_i, seqs, width), BF16),
            pltpu.VMEM((n_pb, cells, pwidth), BF16),
            pltpu.VMEM((n_pb, rows_i * seqs, width), BF16),
            pltpu.VMEM((n_pb, rows_i * seqs, width), BF16),
            pltpu.VMEM((n_pb, rows_i * seqs, width), BF16),
            pltpu.VMEM((n_pb * eparts * seqs, rows_i * LANES), BF16),
            pltpu.VMEM((msg_rows, LANES), BF16),
            pltpu.VMEM((n_src, n_pb, msg_rows, LANES), BF16),
            pltpu.VMEM((TRI_HEADS * cols, residues), F32),
            pltpu.VMEM((n_pb, cells, pwidth), F32),
            pltpu.VMEM((n_pb, cells, 2 * pwidth), BF16),
            pltpu.VMEM(arrays["tensor"].shape, F32),
            pltpu.VMEM(arrays["tensor"].shape, BF16),
            pltpu.VMEM((max(cells * SUBLANES, msg_rows), LANES), F32),
            dma((len(inputs),)),
            dma((n_pb,)),
            dma((n_pb,)),
            dma((n_pb,)),
            dma((n_pb,)),
            dma((n_a,)),
            dma((n_as * n_pb,)),
            dma((n_as * mates,)),
            dma((n_src,)),
        ],
        compiler_params=pltpu.CompilerParams(
            collective_id=0, has_side_effects=True, vmem_limit_bytes=56 * 1024 * 1024
        ),
    )(x_t, *inputs)
    return jnp.transpose(msa, (1, 0, 2)), pair_out.reshape(rows_i, cols, pwidth)


def solution(mesh):
    n_row, n_br, n_pb = mesh.shape["row"], mesh.shape["br"], mesh.shape["pb"]
    n_b = 2 if n_row % (2 * n_pb) == 0 else 1
    sizes = (n_pb, n_row // n_b, n_b, n_br)
    return jax.shard_map(
        functools.partial(on_device, sizes),
        mesh=mesh,
        in_specs=(
            P(("grp", "pb"), ("row", "br"), None),
            P(("grp", "row", "br"), "pb", None),
            P("grp"),
            P("grp"),
            P("grp"),
        )
        + (P(),) * 12,
        out_specs=(P(("grp", "pb"), ("row", "br"), None), P(("grp", "row", "br"), "pb", None)),
        check_vma=False,
    )
```

time: 34.9 us -> 22.9 us (0.66)
  the two profiles are of different devices: /device:TPU:25 before, /device:TPU:0 now
where the time goes in v2:
time: 22.9 us; the launch traced here: 22.7 us
  Pallas kernels  18.2 us (79%)
  local copies, waits for them, and re-layouts  3.86 us (17%)
  between operations  0.65 us (3%)
    pallas_call x1, Pallas kernels, on_device(): pl.pallas_call(functools.partial(kernel, sizes), out_shape=(jax.ShapeDtyp...  18.2 us
    unnamed x5, local copies, waits for them, and re-layouts  3.86 us

profile of v2, /device:TPU:0, one launch (start us, length us, event | category | flops | bytes accessed | tf_op | source)
XLA Modules:
  0.0 22.7 jit_solution(11490935257024449609)
XLA Ops:
  0.6 1.6 %copy.22 = bf16[64,4,256]{2,0,1:T(8,128)(2,1)} copy(bf16[64,4,256]{2,1,0:T(4,128)(2,1)} %param.17) | data formatting | bytes 262144 | tf_op args[0]
  2.2 18.2 %shard_map.176 = (bf16[4,64,256]{2,1,0:T(8,128)(2,1)}, bf16[128,128]{1,0:T(8,128)(2,1)}) custom-call(bf16[4,64,256]{2,1,0:T(8,128)(2,1)} %bitcast.11, s32[1,128]{1,0:T(1,128)} %bitcast.18, bf16[64,256]{1,0:T(8,128)(2,1)} %bitcast.13, s32[1,64]{1,0:T(1,128)} %bitcast.16, s32[64]{0:T(128)} %refs_4_.1, bf16[65,128]{1,0:T(8,128)(2,1)} %refs_5_.1, ...), custom_call_target="tpu_custom_call" | custom-call | tf_op jit(solution)/shard_map/pallas_call | solution.py:389
  20.4 0.0 copy-start
  20.4 1.7 %copy.20 = bf16[64,4,256]{2,1,0:T(4,128)(2,1)} copy(bf16[64,4,256]{2,0,1:T(8,128)(2,1)} %bitcast.12) | data formatting | bytes 262144
  22.1 0.0 copy-done
  22.1 0.6 %copy.24 = bf16[4,32,128]{2,1,0:T(8,128)(2,1)} copy(bf16[4,32,128]{2,1,0:T(8,128)(2,1)S(1)} %bitcast.15) | data formatting | bytes 65536
Async XLA Ops:
  20.4 1.7 %copy-start = (bf16[128,128]{1,0:T(8,128)(2,1)S(1)}, bf16[128,128]{1,0:T(8,128)(2,1)}, u32[]{:S(2)}) copy-start(bf16[128,128]{1,0:T(8,128)(2,1)} %get-tuple-element.5) | copy-start | bytes 98308

commit v3 on v2

--- a/solution.py
+++ b/solution.py
@@ -26,7 +26,7 @@
 
 
 INPUTS = (
-    "chain", "duo", "positions", "scalars", "rel", "pair", "tbias", "qkvg", "tri", "tensor",
+    "x", "chain", "duo", "positions", "scalars", "rel", "pair", "tbias", "qkvg", "tri", "tensor",
     "vproj", "expand", "contract", "resolved", "tout", "up", "down",
 )
 
@@ -72,16 +72,17 @@
     return total
 
 
-def kernel(sizes, *refs):
+def kernel(sizes, shape, *refs):
     n_pb, n_a, n_b, n_c = sizes
-    x_ref = refs[0]
-    hbm = dict(zip(INPUTS, refs[1 : 1 + len(INPUTS)]))
-    out_msa, out_pair = refs[1 + len(INPUTS) : 3 + len(INPUTS)]
-    w = dict(zip(INPUTS, refs[3 + len(INPUTS) : 3 + 2 * len(INPUTS)]))
+    count = len(INPUTS)
+    hbm = dict(zip(INPUTS, refs[:count]))
+    out_msa, out_pair = refs[count : 2 + count]
+    w = dict(zip(INPUTS, refs[2 + count : 2 + 2 * count]))
     (xg, pg, xn_s, k_s, v_s, left_s, msg_s, gather, bias_s, pairin_s, tkv_s, wf_s, wp_s, opm_s,
-     wsem, sx, rx, sp, rp, s1, r1, s2, r2) = refs[3 + 2 * len(INPUTS) :]
-    pair_ref = w["pair"]
-    rows_i, seqs, width = x_ref.shape
+     flat_s, msa_s, pair_s, wsem, sx, rx, sp, rp, s1, r1, s2, r2) = refs[2 + 2 * count :]
+    x_ref, pair_ref = w["x"], w["pair"]
+    rows_i, seqs, width = shape
+    tiles = width // LANES
     cells, pwidth = pair_ref.shape
     cols = cells // rows_i
     residues = w["resolved"].shape[1]
@@ -121,8 +122,21 @@
             barrier, inc=1, device_id=device(a_me, (b_me + db) % n_b, (c_me + dc) % n_c, p_me), device_id_type=MESH
         )
 
-    x_own = x_ref[...].reshape(rows_i * seqs, width)
-    xn_own = normalize(x_own.astype(F32))
+    def by_residue(block):
+        flat_s[...] = block.astype(F32)
+        return jnp.concatenate(
+            [
+                jnp.concatenate(
+                    [flat_s[pl.ds(t * rows_i + r, seqs, stride=tiles * rows_i), :] for t in range(tiles)], axis=1
+                )
+                for r in range(rows_i)
+            ],
+            axis=0,
+        )
+
+    loads["x"].wait()
+    x_own = by_residue(x_ref[...])
+    xn_own = normalize(x_own)
     xn_s[p_me] = xn_own
     loads["chain"].wait()
     loads["duo"].wait()
@@ -261,7 +275,7 @@
         exchange[n_pb - slot - 1][1].wait_recv()
     for d in range(1, n_pb):
         p = (p_me + d) % n_pb
-        xn = normalize(xg[d].reshape(rows_i * seqs, width).astype(F32))
+        xn = normalize(by_residue(xg[d]))
         xn_s[p] = xn
         kv = matmul(xn, w["qkvg"][:, width : 3 * width])
         k_s[p] = kv[:, :width].astype(BF16)
@@ -289,12 +303,19 @@
         mixed.append((gate[span] * head_merge(weighted, VERTICAL_ATTENDS)).astype(BF16))
 
     loads["vproj"].wait()
-    mid = x_own.astype(F32) + matmul(jnp.concatenate(mixed, axis=0), w["vproj"][...])
+    mid = x_own + matmul(jnp.concatenate(mixed, axis=0), w["vproj"][...])
     loads["expand"].wait()
     hidden = jnp.maximum(matmul(normalize(mid), w["expand"][...]), 0.0).astype(BF16)
     loads["contract"].wait()
     fresh = mid + matmul(hidden, w["contract"][...])
-    out_msa[...] = fresh.astype(BF16).reshape(out_msa.shape)
+    for r in range(rows_i):
+        for t in range(tiles):
+            flat_s[pl.ds(t * rows_i + r, seqs, stride=tiles * rows_i), :] = fresh[
+                r * seqs : (r + 1) * seqs, t * LANES : (t + 1) * LANES
+            ]
+    msa_s[...] = flat_s[...].astype(BF16)
+    msa_out = pltpu.make_async_copy(msa_s, out_msa, wsem.at[count])
+    msa_out.start()
 
     for a in range(n_as):
         for db, dc in mates:
@@ -347,8 +368,12 @@
     loads["up"].wait()
     pair_hidden = jnp.maximum(matmul(normalize(pair_mid), w["up"][...]), 0.0).astype(BF16)
     loads["down"].wait()
-    out_pair[...] = (pair_mid + matmul(pair_hidden, w["down"][...])).astype(BF16)
-
+    pair_s[...] = (pair_mid + matmul(pair_hidden, w["down"][...])).astype(BF16)
+    pair_out = pltpu.make_async_copy(pair_s, out_pair, wsem.at[count + 1])
+    pair_out.start()
+
+    msa_out.wait()
+    pair_out.wait()
     for copies in exchange:
         for copy in copies:
             copy.wait_send()
@@ -373,6 +398,8 @@
     arrays = dict(zip(WEIGHTS, weights))
     arrays["duo"] = arrays["duo"].T
     arrays["tbias"] = arrays["tbias"].T
+    tiles = width // LANES
+    arrays["x"] = x.reshape(seqs, rows_i, tiles, LANES).transpose(0, 2, 1, 3).reshape(-1, LANES)
     arrays["pair"] = pair.reshape(cells, pwidth)
     arrays["chain"] = chain.reshape(1, chains)
     arrays["resolved"] = resolved.reshape(1, residues)
@@ -383,22 +410,20 @@
     eparts = factor // SUBLANES
     msg_rows = eparts * seqs // LANES * rows_i * SUBLANES + rows_i * TRI_HEADS
     mates = n_b * n_c - 1
-    vmem = pl.BlockSpec(memory_space=pltpu.VMEM)
     dma = pltpu.SemaphoreType.DMA
-    x_t = jnp.transpose(x, (1, 0, 2))
     msa, pair_out = pl.pallas_call(
-        functools.partial(kernel, sizes),
+        functools.partial(kernel, sizes, (rows_i, seqs, width)),
         out_shape=(
-            jax.ShapeDtypeStruct((rows_i, seqs, width), BF16),
+            jax.ShapeDtypeStruct(arrays["x"].shape, BF16),
             jax.ShapeDtypeStruct((cells, pwidth), BF16),
         ),
-        in_specs=[vmem] + [pl.BlockSpec(memory_space=pltpu.HBM)] * len(inputs),
-        out_specs=(vmem, vmem),
+        in_specs=[pl.BlockSpec(memory_space=pltpu.HBM)] * len(inputs),
+        out_specs=(pl.BlockSpec(memory_space=pltpu.HBM),) * 2,
         scratch_shapes=[
             (pltpu.SMEM if name == "scalars" else pltpu.VMEM)(v.shape, v.dtype) for name, v in zip(INPUTS, inputs)
         ]
         + [
-            pltpu.VMEM((n_pb, rows_i, seqs, width), BF16),
+            pltpu.VMEM((n_pb,) + arrays["x"].shape, BF16),
             pltpu.VMEM((n_pb, cells, pwidth), BF16),
             pltpu.VMEM((n_pb, rows_i * seqs, width), BF16),
             pltpu.VMEM((n_pb, rows_i * seqs, width), BF16),
@@ -412,7 +437,10 @@
             pltpu.VMEM(arrays["tensor"].shape, F32),
             pltpu.VMEM(arrays["tensor"].shape, BF16),
             pltpu.VMEM((max(cells * SUBLANES, msg_rows), LANES), F32),
-            dma((len(inputs),)),
+            pltpu.VMEM(arrays["x"].shape, F32),
+            pltpu.VMEM(arrays["x"].shape, BF16),
+            pltpu.VMEM((cells, pwidth), BF16),
+            dma((len(inputs) + 2,)),
             dma((n_pb,)),
             dma((n_pb,)),
             dma((n_pb,)),
@@ -425,8 +453,9 @@
         compiler_params=pltpu.CompilerParams(
             collective_id=0, has_side_effects=True, vmem_limit_bytes=56 * 1024 * 1024
         ),
-    )(x_t, *inputs)
-    return jnp.transpose(msa, (1, 0, 2)), pair_out.reshape(rows_i, cols, pwidth)
+    )(*inputs)
+    msa = msa.reshape(seqs, tiles, rows_i, LANES).transpose(0, 2, 1, 3).reshape(x.shape)
+    return msa, pair_out.reshape(rows_i, cols, pwidth)
 
 
 def solution(mesh):

time: 22.9 us -> 20.4 us (0.89)
  local copies, waits for them, and re-layouts: 3.86 us -> 2.23 us
  Pallas kernels: 18.2 us -> 17.3 us
    unnamed x5 -> x4, local copies, waits for them, and re-layouts: 3.86 us -> 2.23 us
    pallas_call x1, Pallas kernels: 18.2 us -> 17.3 us  [on_device(): pl.pallas_call(functools.partial(kernel, sizes, (rows_i, seqs, width)), o...]
where the time goes in v3:
time: 20.4 us; the launch traced here: 20.2 us
  Pallas kernels  17.3 us (85%)
  local copies, waits for them, and re-layouts  2.23 us (11%)
  between operations  0.65 us (3%)
    pallas_call x1, Pallas kernels, on_device(): pl.pallas_call(functools.partial(kernel, sizes, (rows_i, seqs, width)), o...  17.3 us
    unnamed x4, local copies, waits for them, and re-layouts  2.23 us

profile of v3, /device:TPU:0, one launch (start us, length us, event | category | flops | bytes accessed | tf_op | source)
XLA Modules:
  0.0 20.2 jit_solution(16724828375409998160)
XLA Ops:
  0.6 17.3 %shard_map.176 = (bf16[512,128]{1,0:T(8,128)(2,1)}, bf16[128,128]{1,0:T(8,128)(2,1)}) custom-call(bf16[512,128]{1,0:T(8,128)(2,1)} %bitcast.17, s32[1,128]{1,0:T(1,128)} %bitcast.24, bf16[64,256]{1,0:T(8,128)(2,1)} %bitcast.19, s32[1,64]{1,0:T(1,128)} %bitcast.22, s32[64]{0:T(128)} %refs_4_.1, bf16[65,128]{1,0:T(8,128)(2,1)} %refs_5_.1, ...), custom_call_target="tpu_custom_call" | custom-call | tf_op jit(solution)/shard_map/pallas_call | solution.py:414
  18.0 0.0 copy-start
  18.0 1.6 %copy.23 = bf16[64,4,256]{2,1,0:T(4,128)(2,1)} copy(bf16[64,4,256]{2,1,0:T(4,128)(2,1)} %bitcast.18) | data formatting | bytes 262144
  19.6 0.0 copy-done
  19.6 0.6 %copy.24 = bf16[4,32,128]{2,1,0:T(8,128)(2,1)} copy(bf16[4,32,128]{2,1,0:T(8,128)(2,1)S(1)} %bitcast.21) | data formatting | bytes 65536
Async XLA Ops:
  18.0 1.6 %copy-start = (bf16[128,128]{1,0:T(8,128)(2,1)S(1)}, bf16[128,128]{1,0:T(8,128)(2,1)}, u32[]{:S(2)}) copy-start(bf16[128,128]{1,0:T(8,128)(2,1)} %get-tuple-element.5) | copy-start | bytes 98308

commit v4 on v3

--- a/solution.py
+++ b/solution.py
@@ -79,7 +79,7 @@
     out_msa, out_pair = refs[count : 2 + count]
     w = dict(zip(INPUTS, refs[2 + count : 2 + 2 * count]))
     (xg, pg, xn_s, k_s, v_s, left_s, msg_s, gather, bias_s, pairin_s, tkv_s, wf_s, wp_s, opm_s,
-     flat_s, msa_s, pair_s, wsem, sx, rx, sp, rp, s1, r1, s2, r2) = refs[2 + 2 * count :]
+     flat_s, msa_s, pair_s, wsem, sx, rx, sp, rp, bt_s, bmsg_s, bgather, s1, r1, s2, r2, sb1, rb1, sb2, rb2) = refs[2 + 2 * count :]
     x_ref, pair_ref = w["x"], w["pair"]
     rows_i, seqs, width = shape
     tiles = width // LANES
@@ -92,7 +92,6 @@
     eparts = factor // SUBLANES
     seq_blocks = eparts * seqs // LANES
     factor_rows = rows_i * SUBLANES
-    base = seq_blocks * factor_rows
 
     grp = lax.axis_index("grp")
     row = lax.axis_index("row")
@@ -121,6 +120,24 @@
         pl.semaphore_signal(
             barrier, inc=1, device_id=device(a_me, (b_me + db) % n_b, (c_me + dc) % n_c, p_me), device_id_type=MESH
         )
+
+    pl.semaphore_wait(barrier, len(line) + len(mates))
+
+    exchange = []
+    for d in range(1, n_pb):
+        peer = device(a_me, b_me, c_me, (p_me + d) % n_pb)
+        exchange.append((
+            pltpu.make_async_remote_copy(
+                src_ref=hbm["pair"], dst_ref=pg.at[n_pb - d], send_sem=sp.at[d], recv_sem=rp.at[n_pb - d],
+                device_id=peer, device_id_type=MESH),
+            pltpu.make_async_remote_copy(
+                src_ref=hbm["x"], dst_ref=xg.at[n_pb - d], send_sem=sx.at[d], recv_sem=rx.at[n_pb - d],
+                device_id=peer, device_id_type=MESH),
+        ))
+    for copy, _ in exchange:
+        copy.start()
+    for _, copy in exchange:
+        copy.start()
 
     def by_residue(block):
         flat_s[...] = block.astype(F32)
@@ -153,6 +170,55 @@
             at = b * factor_rows + j * SUBLANES
             opm_s[at : at + SUBLANES, :] = parts[:, b * LANES : (b + 1) * LANES]
 
+    msg_s[...] = opm_s[: msg_s.shape[0], :].astype(BF16)
+
+    p_to, a_slot = a_me // n_as, a_me % n_as
+    stays = p_to == p_me
+
+    def slot_of(a, b, c):
+        return (a * n_b + b) * n_c + c
+
+    def first(d):
+        return pltpu.make_async_remote_copy(
+            src_ref=msg_s, dst_ref=gather.at[slot_of(a_slot, b_me, c_me), p_me], send_sem=s1.at[d],
+            recv_sem=r1.at[a_slot * n_pb + p_me], device_id=device((a_me + d) % n_a, b_me, c_me, p_to),
+            device_id_type=MESH)
+
+    def first_bias(d):
+        return pltpu.make_async_remote_copy(
+            src_ref=bmsg_s, dst_ref=bgather.at[b_me, c_me, a_slot, p_me], send_sem=sb1.at[d],
+            recv_sem=rb1.at[a_slot * n_pb + p_me], device_id=device((a_me + d) % n_a, b_me, c_me, p_to),
+            device_id_type=MESH)
+
+    def second(da, dp, m):
+        a, p = (a_slot + da) % n_as, (p_me + dp) % n_pb
+        slot = slot_of(a, b_me, c_me)
+        db, dc = mates[m]
+        return pltpu.make_async_remote_copy(
+            src_ref=gather.at[slot, p], dst_ref=gather.at[slot, p],
+            send_sem=s2.at[(da * n_pb + dp) * len(mates) + m], recv_sem=r2.at[slot * n_pb + p],
+            device_id=device(a_me, (b_me + db) % n_b, (c_me + dc) % n_c, p_me), device_id_type=MESH)
+
+    def second_bias(m):
+        db, dc = mates[m]
+        return pltpu.make_async_remote_copy(
+            src_ref=bgather.at[b_me, c_me], dst_ref=bgather.at[b_me, c_me], send_sem=sb2.at[m],
+            recv_sem=rb2.at[b_me * n_c + c_me],
+            device_id=device(a_me, (b_me + db) % n_b, (c_me + dc) % n_c, p_me), device_id_type=MESH)
+
+    for d in range(1, n_a):
+        first(d).start()
+
+    @pl.when(jnp.logical_not(stays))
+    def _():
+        first(0).start()
+
+    @pl.when(stays)
+    def _():
+        gather[slot_of(a_slot, b_me, c_me), p_me] = msg_s[...]
+        for m in range(len(mates)):
+            second(0, 0, m).start()
+
     row_first = (row * n_c + c_me) * rows_i
     bins = 2 * RELPOS_MAX + 1
     loads["positions"].wait()
@@ -169,52 +235,22 @@
     pn_own = normalize(pair_in)
     loads["tbias"].wait()
     bt = matmul_nt(w["tbias"][...], pn_own)
+    bt_s[...] = jnp.zeros_like(bt_s)
     for i in range(rows_i):
         for h in range(TRI_HEADS):
-            at = base + h * rows_i + i
-            opm_s[at : at + 1, :cols] = bt[h : h + 1, i * cols : (i + 1) * cols]
-    msg_s[...] = opm_s[: msg_s.shape[0], :].astype(BF16)
-
-    pl.semaphore_wait(barrier, len(line) + len(mates))
-
-    p_to, a_slot = a_me // n_as, a_me % n_as
-    stays = p_to == p_me
-
-    def slot_of(a, b, c):
-        return (a * n_b + b) * n_c + c
-
-    def first(d):
-        return pltpu.make_async_remote_copy(
-            src_ref=msg_s, dst_ref=gather.at[slot_of(a_slot, b_me, c_me), p_me], send_sem=s1.at[d],
-            recv_sem=r1.at[a_slot * n_pb + p_me], device_id=device((a_me + d) % n_a, b_me, c_me, p_to),
-            device_id_type=MESH)
-
+            at = h * rows_i + i
+            bt_s[at : at + 1, :cols] = bt[h : h + 1, i * cols : (i + 1) * cols]
+    bmsg_s[...] = bt_s[...].astype(BF16)
     for d in range(1, n_a):
-        first(d).start()
+        first_bias(d).start()
 
     @pl.when(jnp.logical_not(stays))
     def _():
-        first(0).start()
+        first_bias(0).start()
 
     @pl.when(stays)
     def _():
-        gather[slot_of(a_slot, b_me, c_me), p_me] = msg_s[...]
-
-    exchange = []
-    for d in range(1, n_pb):
-        peer = device(a_me, b_me, c_me, (p_me + d) % n_pb)
-        exchange.append((
-            pltpu.make_async_remote_copy(
-                src_ref=pair_ref, dst_ref=pg.at[n_pb - d], send_sem=sp.at[d], recv_sem=rp.at[n_pb - d],
-                device_id=peer, device_id_type=MESH),
-            pltpu.make_async_remote_copy(
-                src_ref=x_ref, dst_ref=xg.at[n_pb - d], send_sem=sx.at[d], recv_sem=rx.at[n_pb - d],
-                device_id=peer, device_id_type=MESH),
-        ))
-    for copy, _ in exchange:
-        copy.start()
-    for _, copy in exchange:
-        copy.start()
+        bgather[b_me, c_me, a_slot, p_me] = bmsg_s[...]
 
     loads["qkvg"].wait()
     proj = matmul(xn_own, w["qkvg"][...])
@@ -244,32 +280,42 @@
             at = (e * eparts + q) * factor
             wp_s[at : at + factor, :] = wf_s[pl.ds(q * SUBLANES + e, factor, stride=factor), :].astype(BF16)
 
+    def hand_on(da, dp):
+        a, p = (a_slot + da) % n_as, (p_me + dp) % n_pb
+        pltpu.make_async_remote_copy(
+            src_ref=msg_s, dst_ref=gather.at[slot_of(a, b_me, c_me), p], send_sem=s1.at[0],
+            recv_sem=r1.at[a * n_pb + p], device_id=device((a_me + 1) % n_a, b_me, c_me, p_me),
+            device_id_type=MESH).wait_recv()
+        for m in range(len(mates)):
+            second(da, dp, m).start()
+
+    def bias_in(da, dp):
+        a, p = (a_slot + da) % n_as, (p_me + dp) % n_pb
+        pltpu.make_async_remote_copy(
+            src_ref=bmsg_s, dst_ref=bgather.at[b_me, c_me, a, p], send_sem=sb1.at[0],
+            recv_sem=rb1.at[a * n_pb + p], device_id=device((a_me + 1) % n_a, b_me, c_me, p_me),
+            device_id_type=MESH).wait_recv()
+
+    arrivals = [(da, dp) for da in range(n_as) for dp in range(n_pb)]
+    for da, dp in arrivals[1:]:
+        hand_on(da, dp)
+
+    @pl.when(jnp.logical_not(stays))
+    def _():
+        hand_on(0, 0)
+        bias_in(0, 0)
+
+    for da, dp in arrivals[1:]:
+        bias_in(da, dp)
+    for m in range(len(mates)):
+        second_bias(m).start()
+
     for slot in range(1, n_pb):
         exchange[n_pb - slot - 1][0].wait_recv()
     for d in range(1, n_pb):
         p = (p_me + d) % n_pb
         pn = normalize(pairin_s[p] + pg[d].astype(F32))
         tkv_s[p] = matmul(pn, tri_w[:, pwidth : 3 * pwidth]).astype(BF16)
-
-    second = []
-    for a in range(n_as):
-        slot = slot_of(a, b_me, c_me)
-        for p in range(n_pb):
-            here = jnp.logical_and(stays, jnp.logical_and(a_slot == a, p_me == p))
-
-            @pl.when(jnp.logical_not(here))
-            def _():
-                pltpu.make_async_remote_copy(
-                    src_ref=msg_s, dst_ref=gather.at[slot, p], send_sem=s1.at[0], recv_sem=r1.at[a * n_pb + p],
-                    device_id=device((a_me + 1) % n_a, b_me, c_me, p_me), device_id_type=MESH).wait_recv()
-
-        for m, (db, dc) in enumerate(mates):
-            copy = pltpu.make_async_remote_copy(
-                src_ref=gather.at[slot], dst_ref=gather.at[slot], send_sem=s2.at[a * len(mates) + m],
-                recv_sem=r2.at[slot],
-                device_id=device(a_me, (b_me + db) % n_b, (c_me + dc) % n_c, p_me), device_id_type=MESH)
-            copy.start()
-            second.append(copy)
 
     for slot in range(1, n_pb):
         exchange[n_pb - slot - 1][1].wait_recv()
@@ -317,12 +363,39 @@
     msa_out = pltpu.make_async_copy(msa_s, out_msa, wsem.at[count])
     msa_out.start()
 
+    for db, dc in mates:
+        b, c = (b_me + db) % n_b, (c_me + dc) % n_c
+        pltpu.make_async_remote_copy(
+            src_ref=bgather.at[b, c], dst_ref=bgather.at[b, c], send_sem=sb2.at[0], recv_sem=rb2.at[b * n_c + c],
+            device_id=device(a_me, b, c, p_me), device_id_type=MESH).wait_recv()
+    for s in range(n_src):
+        part = jnp.concatenate(
+            [bgather[s // n_c % n_b, s % n_c, s // (n_b * n_c), p].astype(F32)[:, :cols] for p in range(n_pb)], axis=1
+        )
+        for h in range(TRI_HEADS):
+            bias_s[h * cols + s * rows_i : h * cols + (s + 1) * rows_i, :] = part[h * rows_i : (h + 1) * rows_i, :]
+    loads["resolved"].wait()
+    bias = bias_s[...] + (w["resolved"][...].astype(F32) - 1.0) * MASK_NEGATIVE
+    tri_mixed = []
+    for i in range(rows_i):
+        span = slice(i * cols, (i + 1) * cols)
+        keys = jnp.concatenate([tkv_s[p, span, :pwidth] for p in range(n_pb)], axis=0)
+        values = jnp.concatenate([tkv_s[p, span, pwidth:] for p in range(n_pb)], axis=0)
+        scores = matmul_nt(head_stack(tri_q[span], TRI_HEADS), keys) * scale + bias
+        weighted = matmul(softmax_rows(scores), values)
+        tri_mixed.append((tri_gate[span] * head_merge(weighted, TRI_HEADS)).astype(BF16))
+    loads["tout"].wait()
+    tri_update = matmul(jnp.concatenate(tri_mixed, axis=0), w["tout"][...])
+
     for a in range(n_as):
-        for db, dc in mates:
-            slot = slot_of(a, (b_me + db) % n_b, (c_me + dc) % n_c)
-            pltpu.make_async_remote_copy(
-                src_ref=gather.at[slot], dst_ref=gather.at[slot], send_sem=s2.at[0], recv_sem=r2.at[slot],
-                device_id=device(a_me, (b_me + db) % n_b, (c_me + dc) % n_c, p_me), device_id_type=MESH).wait_recv()
+        for p in range(n_pb):
+            for db, dc in mates:
+                b, c = (b_me + db) % n_b, (c_me + dc) % n_c
+                slot = slot_of(a, b, c)
+                pltpu.make_async_remote_copy(
+                    src_ref=gather.at[slot, p], dst_ref=gather.at[slot, p], send_sem=s2.at[0],
+                    recv_sem=r2.at[slot * n_pb + p], device_id=device(a_me, b, c, p_me),
+                    device_id_type=MESH).wait_recv()
 
     right_all = jnp.concatenate(
         [
@@ -347,24 +420,7 @@
     )
     opm = matmul(lhs, wp_s[...]) / jnp.sum(chain)
 
-    for s in range(n_src):
-        part = jnp.concatenate(
-            [gather[s, p, base : base + rows_i * TRI_HEADS, :].astype(F32)[:, :cols] for p in range(n_pb)], axis=1
-        )
-        for h in range(TRI_HEADS):
-            bias_s[h * cols + s * rows_i : h * cols + (s + 1) * rows_i, :] = part[h * rows_i : (h + 1) * rows_i, :]
-    loads["resolved"].wait()
-    bias = bias_s[...] + (w["resolved"][...].astype(F32) - 1.0) * MASK_NEGATIVE
-    tri_mixed = []
-    for i in range(rows_i):
-        span = slice(i * cols, (i + 1) * cols)
-        keys = jnp.concatenate([tkv_s[p, span, :pwidth] for p in range(n_pb)], axis=0)
-        values = jnp.concatenate([tkv_s[p, span, pwidth:] for p in range(n_pb)], axis=0)
-        scores = matmul_nt(head_stack(tri_q[span], TRI_HEADS), keys) * scale + bias
-        weighted = matmul(softmax_rows(scores), values)
-        tri_mixed.append((tri_gate[span] * head_merge(weighted, TRI_HEADS)).astype(BF16))
-    loads["tout"].wait()
-    pair_mid = pair_in + matmul(jnp.concatenate(tri_mixed, axis=0), w["tout"][...]) + opm
+    pair_mid = pair_in + tri_update + opm
     loads["up"].wait()
     pair_hidden = jnp.maximum(matmul(normalize(pair_mid), w["up"][...]), 0.0).astype(BF16)
     loads["down"].wait()
@@ -377,14 +433,29 @@
     for copies in exchange:
         for copy in copies:
             copy.wait_send()
-    for copy in second:
-        copy.wait_send()
+    for m in range(len(mates)):
+        for da, dp in arrivals:
+            second(da, dp, m).wait_send()
+        second_bias(m).wait_send()
     for d in range(1, n_a):
         first(d).wait_send()
+        first_bias(d).wait_send()
 
     @pl.when(jnp.logical_not(stays))
     def _():
         first(0).wait_send()
+        first_bias(0).wait_send()
+
+
+def finish(msa_ref, pair_ref, out_msa, out_pair, sem):
+    copies = [
+        pltpu.make_async_copy(msa_ref, out_msa, sem.at[0]),
+        pltpu.make_async_copy(pair_ref, out_pair, sem.at[1]),
+    ]
+    for copy in copies:
+        copy.start()
+    for copy in copies:
+        copy.wait()
 
 
 def on_device(sizes, x, pair, chain, resolved, positions, *weights):
@@ -408,8 +479,9 @@
     inputs = [arrays[name] for name in INPUTS]
     factor = arrays["duo"].shape[0] // 2
     eparts = factor // SUBLANES
-    msg_rows = eparts * seqs // LANES * rows_i * SUBLANES + rows_i * TRI_HEADS
+    msg_rows = eparts * seqs // LANES * rows_i * SUBLANES
     mates = n_b * n_c - 1
+    cols_padded = -(-cols // LANES) * LANES
     dma = pltpu.SemaphoreType.DMA
     msa, pair_out = pl.pallas_call(
         functools.partial(kernel, sizes, (rows_i, seqs, width)),
@@ -445,15 +517,34 @@
             dma((n_pb,)),
             dma((n_pb,)),
             dma((n_pb,)),
+            pltpu.VMEM((rows_i * TRI_HEADS, cols_padded), F32),
+            pltpu.VMEM((rows_i * TRI_HEADS, cols_padded), BF16),
+            pltpu.VMEM((n_b, n_c, n_as, n_pb, rows_i * TRI_HEADS, cols_padded), BF16),
             dma((n_a,)),
             dma((n_as * n_pb,)),
-            dma((n_as * mates,)),
-            dma((n_src,)),
+            dma((n_as * n_pb * mates,)),
+            dma((n_src * n_pb,)),
+            dma((n_a,)),
+            dma((n_as * n_pb,)),
+            dma((mates,)),
+            dma((n_b * n_c,)),
         ],
         compiler_params=pltpu.CompilerParams(
             collective_id=0, has_side_effects=True, vmem_limit_bytes=56 * 1024 * 1024
         ),
     )(*inputs)
+    hbm = pl.BlockSpec(memory_space=pltpu.HBM)
+    msa, pair_out = pl.pallas_call(
+        finish,
+        out_shape=(
+            jax.ShapeDtypeStruct(msa.shape, BF16),
+            jax.ShapeDtypeStruct(pair_out.shape, BF16),
+        ),
+        in_specs=[hbm] * 2,
+        out_specs=(hbm, hbm),
+        scratch_shapes=[dma((2,))],
+        compiler_params=pltpu.CompilerParams(vmem_limit_bytes=56 * 1024 * 1024),
+    )(msa, pair_out)
     msa = msa.reshape(seqs, tiles, rows_i, LANES).transpose(0, 2, 1, 3).reshape(x.shape)
     return msa, pair_out.reshape(rows_i, cols, pwidth)
 

time: 20.4 us -> 26.7 us (1.31)
  Pallas kernels: 17.3 us -> 25.9 us
  local copies, waits for them, and re-layouts: 2.23 us -> 0 us
    pallas_call x0 -> x1, Pallas kernels: none -> 6.08 us  [on_device(): pl.pallas_call(finish, out_shape=(jax.ShapeDtypeStruct(msa.shape, BF16),...]
    pallas_call x1, Pallas kernels: 17.3 us -> 19.9 us  [on_device(): pl.pallas_call(functools.partial(kernel, sizes, (rows_i, seqs, width)), o...]
    unnamed x4 -> x0, local copies, waits for them, and re-layouts: 2.23 us -> none
where the time goes in v4:
time: 26.7 us; the launch traced here: 26.6 us
  Pallas kernels  25.9 us (97%)
  between operations  0.65 us (2%)
    pallas_call x1, Pallas kernels, on_device(): pl.pallas_call(functools.partial(kernel, sizes, (rows_i, seqs, width)), o...  19.9 us
    pallas_call x1, Pallas kernels, on_device(): pl.pallas_call(finish, out_shape=(jax.ShapeDtypeStruct(msa.shape, BF16),...  6.08 us

profile of v4, /device:TPU:0, one launch (start us, length us, event | category | flops | bytes accessed | tf_op | source)
XLA Modules:
  0.0 26.6 jit_solution(1312322922617063679)
XLA Ops:
  0.6 19.9 %shard_map.176 = (bf16[512,128]{1,0:T(8,128)(2,1)}, bf16[128,128]{1,0:T(8,128)(2,1)}) custom-call(bf16[512,128]{1,0:T(8,128)(2,1)} %bitcast.17, s32[1,128]{1,0:T(1,128)} %bitcast.22, bf16[64,256]{1,0:T(8,128)(2,1)} %bitcast.18, s32[1,64]{1,0:T(1,128)} %bitcast.20, s32[64]{0:T(128)} %refs_4_.1, bf16[65,128]{1,0:T(8,128)(2,1)} %refs_5_.1, ...), custom_call_target="tpu_custom_call" | custom-call | tf_op jit(solution)/shard_map/pallas_call | solution.py:486
  20.5 6.1 %shard_map.177 = (bf16[512,128]{1,0:T(8,128)(2,1)}, bf16[128,128]{1,0:T(8,128)(2,1)}) custom-call(bf16[512,128]{1,0:T(8,128)(2,1)} %get-tuple-element.6.msa_ref, bf16[128,128]{1,0:T(8,128)(2,1)} %get-tuple-element.7.pair_ref), custom_call_target="tpu_custom_call" | custom-call | tf_op jit(solution)/shard_map/pallas_call | solution.py:537

commit v5 on v4

--- a/solution.py
+++ b/solution.py
@@ -121,24 +121,6 @@
             barrier, inc=1, device_id=device(a_me, (b_me + db) % n_b, (c_me + dc) % n_c, p_me), device_id_type=MESH
         )
 
-    pl.semaphore_wait(barrier, len(line) + len(mates))
-
-    exchange = []
-    for d in range(1, n_pb):
-        peer = device(a_me, b_me, c_me, (p_me + d) % n_pb)
-        exchange.append((
-            pltpu.make_async_remote_copy(
-                src_ref=hbm["pair"], dst_ref=pg.at[n_pb - d], send_sem=sp.at[d], recv_sem=rp.at[n_pb - d],
-                device_id=peer, device_id_type=MESH),
-            pltpu.make_async_remote_copy(
-                src_ref=hbm["x"], dst_ref=xg.at[n_pb - d], send_sem=sx.at[d], recv_sem=rx.at[n_pb - d],
-                device_id=peer, device_id_type=MESH),
-        ))
-    for copy, _ in exchange:
-        copy.start()
-    for _, copy in exchange:
-        copy.start()
-
     def by_residue(block):
         flat_s[...] = block.astype(F32)
         return jnp.concatenate(
@@ -206,6 +188,8 @@
             recv_sem=rb2.at[b_me * n_c + c_me],
             device_id=device(a_me, (b_me + db) % n_b, (c_me + dc) % n_c, p_me), device_id_type=MESH)
 
+    pl.semaphore_wait(barrier, len(line) + len(mates))
+
     for d in range(1, n_a):
         first(d).start()
 
@@ -218,6 +202,23 @@
         gather[slot_of(a_slot, b_me, c_me), p_me] = msg_s[...]
         for m in range(len(mates)):
             second(0, 0, m).start()
+
+    exchange = []
+    for d in range(1, n_pb):
+        peer = device(a_me, b_me, c_me, (p_me + d) % n_pb)
+        exchange.append((
+            pltpu.make_async_remote_copy(
+                src_ref=pair_ref, dst_ref=pg.at[n_pb - d], send_sem=sp.at[d], recv_sem=rp.at[n_pb - d],
+                device_id=peer, device_id_type=MESH),
+            pltpu.make_async_remote_copy(
+                src_ref=x_ref, dst_ref=xg.at[n_pb - d], send_sem=sx.at[d], recv_sem=rx.at[n_pb - d],
+                device_id=peer, device_id_type=MESH),
+        ))
+    loads["pair"].wait()
+    for copy, _ in exchange:
+        copy.start()
+    for _, copy in exchange:
+        copy.start()
 
     row_first = (row * n_c + c_me) * rows_i
     bins = 2 * RELPOS_MAX + 1
@@ -230,7 +231,6 @@
         added = matmul_tn(jnp.where(hot, 1.0, 0.0).astype(BF16), w["rel"][...])
         for p in range(n_pb):
             pairin_s[p, i * cols : (i + 1) * cols] = added[p * cols : (p + 1) * cols]
-    loads["pair"].wait()
     pair_in = pairin_s[p_me] + pair_ref[...].astype(F32)
     pn_own = normalize(pair_in)
     loads["tbias"].wait()
@@ -359,9 +359,7 @@
             flat_s[pl.ds(t * rows_i + r, seqs, stride=tiles * rows_i), :] = fresh[
                 r * seqs : (r + 1) * seqs, t * LANES : (t + 1) * LANES
             ]
-    msa_s[...] = flat_s[...].astype(BF16)
-    msa_out = pltpu.make_async_copy(msa_s, out_msa, wsem.at[count])
-    msa_out.start()
+    out_msa[...] = flat_s[...].astype(BF16)
 
     for db, dc in mates:
         b, c = (b_me + db) % n_b, (c_me + dc) % n_c
@@ -424,12 +422,8 @@
     loads["up"].wait()
     pair_hidden = jnp.maximum(matmul(normalize(pair_mid), w["up"][...]), 0.0).astype(BF16)
     loads["down"].wait()
-    pair_s[...] = (pair_mid + matmul(pair_hidden, w["down"][...])).astype(BF16)
-    pair_out = pltpu.make_async_copy(pair_s, out_pair, wsem.at[count + 1])
-    pair_out.start()
-
-    msa_out.wait()
-    pair_out.wait()
+    out_pair[...] = (pair_mid + matmul(pair_hidden, w["down"][...])).astype(BF16)
+
     for copies in exchange:
         for copy in copies:
             copy.wait_send()
@@ -486,11 +480,11 @@
     msa, pair_out = pl.pallas_call(
         functools.partial(kernel, sizes, (rows_i, seqs, width)),
         out_shape=(
-            jax.ShapeDtypeStruct(arrays["x"].shape, BF16),
-            jax.ShapeDtypeStruct((cells, pwidth), BF16),
+            pltpu.VMEM(arrays["x"].shape, BF16),
+            pltpu.VMEM((cells, pwidth), BF16),
         ),
         in_specs=[pl.BlockSpec(memory_space=pltpu.HBM)] * len(inputs),
-        out_specs=(pl.BlockSpec(memory_space=pltpu.HBM),) * 2,
+        out_specs=(pl.BlockSpec(memory_space=pltpu.VMEM),) * 2,
         scratch_shapes=[
             (pltpu.SMEM if name == "scalars" else pltpu.VMEM)(v.shape, v.dtype) for name, v in zip(INPUTS, inputs)
         ]
@@ -534,16 +528,17 @@
         ),
     )(*inputs)
     hbm = pl.BlockSpec(memory_space=pltpu.HBM)
+    vmem = pl.BlockSpec(memory_space=pltpu.VMEM)
     msa, pair_out = pl.pallas_call(
         finish,
         out_shape=(
             jax.ShapeDtypeStruct(msa.shape, BF16),
             jax.ShapeDtypeStruct(pair_out.shape, BF16),
         ),
-        in_specs=[hbm] * 2,
+        in_specs=[vmem] * 2,
         out_specs=(hbm, hbm),
         scratch_shapes=[dma((2,))],
-        compiler_params=pltpu.CompilerParams(vmem_limit_bytes=56 * 1024 * 1024),
+        compiler_params=pltpu.CompilerParams(vmem_limit_bytes=8 * 1024 * 1024),
     )(msa, pair_out)
     msa = msa.reshape(seqs, tiles, rows_i, LANES).transpose(0, 2, 1, 3).reshape(x.shape)
     return msa, pair_out.reshape(rows_i, cols, pwidth)

time: 26.7 us -> 19.6 us (0.73)
  Pallas kernels: 25.9 us -> 18.8 us
    pallas_call x1, Pallas kernels: 6.08 us -> 0.68 us  [on_device(): pl.pallas_call(finish, out_shape=(jax.ShapeDtypeStruct(msa.shape, BF16),...]
    pallas_call x1, Pallas kernels: 19.9 us -> 18.1 us  [on_device(): pl.pallas_call(functools.partial(kernel, sizes, (rows_i, seqs, width)), o...]
where the time goes in v5:
time: 19.6 us; the launch traced here: 19.4 us
  Pallas kernels  18.8 us (96%)
  between operations  0.65 us (3%)
    pallas_call x1, Pallas kernels, on_device(): pl.pallas_call(functools.partial(kernel, sizes, (rows_i, seqs, width)), o...  18.1 us
    pallas_call x1, Pallas kernels, on_device(): pl.pallas_call(finish, out_shape=(jax.ShapeDtypeStruct(msa.shape, BF16),...  0.68 us

profile of v5, /device:TPU:0, one launch (start us, length us, event | category | flops | bytes accessed | tf_op | source)
XLA Modules:
  0.0 19.4 jit_solution(3502268865106193630)
XLA Ops:
  0.6 18.1 %shard_map.176 = (bf16[512,128]{1,0:T(8,128)(2,1)S(1)}, bf16[128,128]{1,0:T(8,128)(2,1)S(1)}) custom-call(bf16[512,128]{1,0:T(8,128)(2,1)} %bitcast.17, s32[1,128]{1,0:T(1,128)} %bitcast.22, bf16[64,256]{1,0:T(8,128)(2,1)} %bitcast.18, s32[1,64]{1,0:T(1,128)} %bitcast.20, s32[64]{0:T(128)} %refs_4_.1, bf16[65,128]{1,0:T(8,128)(2,1)} %refs_5_.1, ...), custom_call_target="tpu_custom_call" | custom-call | tf_op jit(solution)/shard_map/pallas_call | solution.py:480
  18.8 0.7 %shard_map.177 = (bf16[512,128]{1,0:T(8,128)(2,1)}, bf16[128,128]{1,0:T(8,128)(2,1)}) custom-call(bf16[512,128]{1,0:T(8,128)(2,1)S(1)} %get-tuple-element.6.msa_ref, bf16[128,128]{1,0:T(8,128)(2,1)S(1)} %get-tuple-element.7.pair_ref), custom_call_target="tpu_custom_call" | custom-call | tf_op jit(solution)/shard_map/pallas_call | solution.py:532

commit v6 on v3

--- a/solution.py
+++ b/solution.py
@@ -78,8 +78,8 @@
     hbm = dict(zip(INPUTS, refs[:count]))
     out_msa, out_pair = refs[count : 2 + count]
     w = dict(zip(INPUTS, refs[2 + count : 2 + 2 * count]))
-    (xg, pg, xn_s, k_s, v_s, left_s, msg_s, gather, bias_s, pairin_s, tkv_s, wf_s, wp_s, opm_s,
-     flat_s, msa_s, pair_s, wsem, sx, rx, sp, rp, s1, r1, s2, r2) = refs[2 + 2 * count :]
+    (xg, pg, k_s, v_s, left_s, msg_s, gather, bias_s, pairin_s, tkv_s, wf_s, wp_s, opm_s,
+     flat_s, wsem, sx, rx, sp, rp, s1, r1, s2, r2) = refs[2 + 2 * count :]
     x_ref, pair_ref = w["x"], w["pair"]
     rows_i, seqs, width = shape
     tiles = width // LANES
@@ -137,7 +137,6 @@
     loads["x"].wait()
     x_own = by_residue(x_ref[...])
     xn_own = normalize(x_own)
-    xn_s[p_me] = xn_own
     loads["chain"].wait()
     loads["duo"].wait()
     chain = w["chain"][...].astype(F32)
@@ -175,47 +174,6 @@
             opm_s[at : at + 1, :cols] = bt[h : h + 1, i * cols : (i + 1) * cols]
     msg_s[...] = opm_s[: msg_s.shape[0], :].astype(BF16)
 
-    pl.semaphore_wait(barrier, len(line) + len(mates))
-
-    p_to, a_slot = a_me // n_as, a_me % n_as
-    stays = p_to == p_me
-
-    def slot_of(a, b, c):
-        return (a * n_b + b) * n_c + c
-
-    def first(d):
-        return pltpu.make_async_remote_copy(
-            src_ref=msg_s, dst_ref=gather.at[slot_of(a_slot, b_me, c_me), p_me], send_sem=s1.at[d],
-            recv_sem=r1.at[a_slot * n_pb + p_me], device_id=device((a_me + d) % n_a, b_me, c_me, p_to),
-            device_id_type=MESH)
-
-    for d in range(1, n_a):
-        first(d).start()
-
-    @pl.when(jnp.logical_not(stays))
-    def _():
-        first(0).start()
-
-    @pl.when(stays)
-    def _():
-        gather[slot_of(a_slot, b_me, c_me), p_me] = msg_s[...]
-
-    exchange = []
-    for d in range(1, n_pb):
-        peer = device(a_me, b_me, c_me, (p_me + d) % n_pb)
-        exchange.append((
-            pltpu.make_async_remote_copy(
-                src_ref=pair_ref, dst_ref=pg.at[n_pb - d], send_sem=sp.at[d], recv_sem=rp.at[n_pb - d],
-                device_id=peer, device_id_type=MESH),
-            pltpu.make_async_remote_copy(
-                src_ref=x_ref, dst_ref=xg.at[n_pb - d], send_sem=sx.at[d], recv_sem=rx.at[n_pb - d],
-                device_id=peer, device_id_type=MESH),
-        ))
-    for copy, _ in exchange:
-        copy.start()
-    for _, copy in exchange:
-        copy.start()
-
     loads["qkvg"].wait()
     proj = matmul(xn_own, w["qkvg"][...])
     query = proj[:, :width].astype(BF16).astype(F32)
@@ -244,6 +202,61 @@
             at = (e * eparts + q) * factor
             wp_s[at : at + factor, :] = wf_s[pl.ds(q * SUBLANES + e, factor, stride=factor), :].astype(BF16)
 
+    left_w = jnp.concatenate([w["duo"][:factor, :]] * eparts, axis=0)
+    lane_part = lax.broadcasted_iota(jnp.int32, (seqs, LANES), 1) // factor
+
+    def put_left(p, xn):
+        left4 = matmul_nt(xn, left_w)
+        for i in range(rows_i):
+            block = left4[i * seqs : (i + 1) * seqs]
+            for q in range(eparts):
+                left_s[p, q * seqs : (q + 1) * seqs, i * LANES : (i + 1) * LANES] = (
+                    jnp.where(lane_part == q, block, 0.0).astype(BF16)
+                )
+
+    put_left(p_me, xn_own)
+
+    pl.semaphore_wait(barrier, len(line) + len(mates))
+
+    p_to, a_slot = a_me // n_as, a_me % n_as
+    stays = p_to == p_me
+
+    def slot_of(a, b, c):
+        return (a * n_b + b) * n_c + c
+
+    def first(d):
+        return pltpu.make_async_remote_copy(
+            src_ref=msg_s, dst_ref=gather.at[slot_of(a_slot, b_me, c_me), p_me], send_sem=s1.at[d],
+            recv_sem=r1.at[a_slot * n_pb + p_me], device_id=device((a_me + d) % n_a, b_me, c_me, p_to),
+            device_id_type=MESH)
+
+    for d in range(1, n_a):
+        first(d).start()
+
+    @pl.when(jnp.logical_not(stays))
+    def _():
+        first(0).start()
+
+    @pl.when(stays)
+    def _():
+        gather[slot_of(a_slot, b_me, c_me), p_me] = msg_s[...]
+
+    exchange = []
+    for d in range(1, n_pb):
+        peer = device(a_me, b_me, c_me, (p_me + d) % n_pb)
+        exchange.append((
+            pltpu.make_async_remote_copy(
+                src_ref=pair_ref, dst_ref=pg.at[n_pb - d], send_sem=sp.at[d], recv_sem=rp.at[n_pb - d],
+                device_id=peer, device_id_type=MESH),
+            pltpu.make_async_remote_copy(
+                src_ref=x_ref, dst_ref=xg.at[n_pb - d], send_sem=sx.at[d], recv_sem=rx.at[n_pb - d],
+                device_id=peer, device_id_type=MESH),
+        ))
+    for copy, _ in exchange:
+        copy.start()
+    for _, copy in exchange:
+        copy.start()
+
     for slot in range(1, n_pb):
         exchange[n_pb - slot - 1][0].wait_recv()
     for d in range(1, n_pb):
@@ -276,21 +289,10 @@
     for d in range(1, n_pb):
         p = (p_me + d) % n_pb
         xn = normalize(by_residue(xg[d]))
-        xn_s[p] = xn
+        put_left(p, xn)
         kv = matmul(xn, w["qkvg"][:, width : 3 * width])
         k_s[p] = kv[:, :width].astype(BF16)
         v_s[p] = kv[:, width:].astype(BF16)
-
-    left_w = jnp.concatenate([w["duo"][:factor, :]] * eparts, axis=0)
-    lane_part = lax.broadcasted_iota(jnp.int32, (seqs, LANES), 1) // factor
-    for p in range(n_pb):
-        left4 = matmul_nt(xn_s[p], left_w)
-        for i in range(rows_i):
-            block = left4[i * seqs : (i + 1) * seqs]
-            for q in range(eparts):
-                left_s[(p * eparts + q) * seqs : (p * eparts + q + 1) * seqs, i * LANES : (i + 1) * LANES] = (
-                    jnp.where(lane_part == q, block, 0.0).astype(BF16)
-                )
 
     seq_bias = (chain - 1.0) * MASK_NEGATIVE
     mixed = []
@@ -313,9 +315,7 @@
             flat_s[pl.ds(t * rows_i + r, seqs, stride=tiles * rows_i), :] = fresh[
                 r * seqs : (r + 1) * seqs, t * LANES : (t + 1) * LANES
             ]
-    msa_s[...] = flat_s[...].astype(BF16)
-    msa_out = pltpu.make_async_copy(msa_s, out_msa, wsem.at[count])
-    msa_out.start()
+    out_msa[...] = flat_s[...].astype(BF16)
 
     for a in range(n_as):
         for db, dc in mates:
@@ -338,7 +338,7 @@
         ],
         axis=0,
     )
-    outer = matmul(right_all, left_s[...])
+    outer = matmul(right_all, left_s[...].reshape(n_pb * eparts * seqs, rows_i * LANES))
     opm_s[: cells * SUBLANES, :] = jnp.concatenate(
         [outer[:, i * LANES : (i + 1) * LANES] for i in range(rows_i)], axis=0
     )
@@ -368,12 +368,8 @@
     loads["up"].wait()
     pair_hidden = jnp.maximum(matmul(normalize(pair_mid), w["up"][...]), 0.0).astype(BF16)
     loads["down"].wait()
-    pair_s[...] = (pair_mid + matmul(pair_hidden, w["down"][...])).astype(BF16)
-    pair_out = pltpu.make_async_copy(pair_s, out_pair, wsem.at[count + 1])
-    pair_out.start()
-
-    msa_out.wait()
-    pair_out.wait()
+    out_pair[...] = (pair_mid + matmul(pair_hidden, w["down"][...])).astype(BF16)
+
     for copies in exchange:
         for copy in copies:
             copy.wait_send()
@@ -385,6 +381,17 @@
     @pl.when(jnp.logical_not(stays))
     def _():
         first(0).wait_send()
+
+
+def finish(msa_ref, pair_ref, out_msa, out_pair, sem):
+    copies = [
+        pltpu.make_async_copy(msa_ref, out_msa, sem.at[0]),
+        pltpu.make_async_copy(pair_ref, out_pair, sem.at[1]),
+    ]
+    for copy in copies:
+        copy.start()
+    for copy in copies:
+        copy.wait()
 
 
 def on_device(sizes, x, pair, chain, resolved, positions, *weights):
@@ -414,11 +421,11 @@
     msa, pair_out = pl.pallas_call(
         functools.partial(kernel, sizes, (rows_i, seqs, width)),
         out_shape=(
-            jax.ShapeDtypeStruct(arrays["x"].shape, BF16),
-            jax.ShapeDtypeStruct((cells, pwidth), BF16),
+            pltpu.VMEM(arrays["x"].shape, BF16),
+            pltpu.VMEM((cells, pwidth), BF16),
         ),
         in_specs=[pl.BlockSpec(memory_space=pltpu.HBM)] * len(inputs),
-        out_specs=(pl.BlockSpec(memory_space=pltpu.HBM),) * 2,
+        out_specs=(pl.BlockSpec(memory_space=pltpu.VMEM),) * 2,
         scratch_shapes=[
             (pltpu.SMEM if name == "scalars" else pltpu.VMEM)(v.shape, v.dtype) for name, v in zip(INPUTS, inputs)
         ]
@@ -427,8 +434,7 @@
             pltpu.VMEM((n_pb, cells, pwidth), BF16),
             pltpu.VMEM((n_pb, rows_i * seqs, width), BF16),
             pltpu.VMEM((n_pb, rows_i * seqs, width), BF16),
-            pltpu.VMEM((n_pb, rows_i * seqs, width), BF16),
-            pltpu.VMEM((n_pb * eparts * seqs, rows_i * LANES), BF16),
+            pltpu.VMEM((n_pb, eparts * seqs, rows_i * LANES), BF16),
             pltpu.VMEM((msg_rows, LANES), BF16),
             pltpu.VMEM((n_src, n_pb, msg_rows, LANES), BF16),
             pltpu.VMEM((TRI_HEADS * cols, residues), F32),
@@ -438,9 +444,7 @@
             pltpu.VMEM(arrays["tensor"].shape, BF16),
             pltpu.VMEM((max(cells * SUBLANES, msg_rows), LANES), F32),
             pltpu.VMEM(arrays["x"].shape, F32),
-            pltpu.VMEM(arrays["x"].shape, BF16),
-            pltpu.VMEM((cells, pwidth), BF16),
-            dma((len(inputs) + 2,)),
+            dma((len(inputs),)),
             dma((n_pb,)),
             dma((n_pb,)),
             dma((n_pb,)),
@@ -454,6 +458,19 @@
             collective_id=0, has_side_effects=True, vmem_limit_bytes=56 * 1024 * 1024
         ),
     )(*inputs)
+    hbm = pl.BlockSpec(memory_space=pltpu.HBM)
+    vmem = pl.BlockSpec(memory_space=pltpu.VMEM)
+    msa, pair_out = pl.pallas_call(
+        finish,
+        out_shape=(
+            jax.ShapeDtypeStruct(msa.shape, BF16),
+            jax.ShapeDtypeStruct(pair_out.shape, BF16),
+        ),
+        in_specs=[vmem] * 2,
+        out_specs=(hbm, hbm),
+        scratch_shapes=[dma((2,))],
+        compiler_params=pltpu.CompilerParams(vmem_limit_bytes=8 * 1024 * 1024),
+    )(msa, pair_out)
     msa = msa.reshape(seqs, tiles, rows_i, LANES).transpose(0, 2, 1, 3).reshape(x.shape)
     return msa, pair_out.reshape(rows_i, cols, pwidth)
 

time: 20.4 us -> 18.2 us (0.89)
  local copies, waits for them, and re-layouts: 2.23 us -> 0 us
    unnamed x4 -> x0, local copies, waits for them, and re-layouts: 2.23 us -> none
    pallas_call x0 -> x1, Pallas kernels: none -> 0.68 us  [on_device(): pl.pallas_call(finish, out_shape=(jax.ShapeDtypeStruct(msa.shape, BF16),...]
    pallas_call x1, Pallas kernels: 17.3 us -> 16.7 us  [on_device(): pl.pallas_call(functools.partial(kernel, sizes, (rows_i, seqs, width)), o...]
where the time goes in v6:
time: 18.2 us; the launch traced here: 18 us
  Pallas kernels  17.4 us (96%)
  between operations  0.65 us (4%)
    pallas_call x1, Pallas kernels, on_device(): pl.pallas_call(functools.partial(kernel, sizes, (rows_i, seqs, width)), o...  16.7 us
    pallas_call x1, Pallas kernels, on_device(): pl.pallas_call(finish, out_shape=(jax.ShapeDtypeStruct(msa.shape, BF16),...  0.68 us

profile of v6, /device:TPU:0, one launch (start us, length us, event | category | flops | bytes accessed | tf_op | source)
XLA Modules:
  0.0 18.0 jit_solution(4305766357756185573)
XLA Ops:
  0.6 16.7 %shard_map.176 = (bf16[512,128]{1,0:T(8,128)(2,1)S(1)}, bf16[128,128]{1,0:T(8,128)(2,1)S(1)}) custom-call(bf16[512,128]{1,0:T(8,128)(2,1)} %bitcast.17, s32[1,128]{1,0:T(1,128)} %bitcast.22, bf16[64,256]{1,0:T(8,128)(2,1)} %bitcast.18, s32[1,64]{1,0:T(1,128)} %bitcast.20, s32[64]{0:T(128)} %refs_4_.1, bf16[65,128]{1,0:T(8,128)(2,1)} %refs_5_.1, ...), custom_call_target="tpu_custom_call" | custom-call | tf_op jit(solution)/shard_map/pallas_call | solution.py:421
  17.3 0.7 %shard_map.177 = (bf16[512,128]{1,0:T(8,128)(2,1)}, bf16[128,128]{1,0:T(8,128)(2,1)}) custom-call(bf16[512,128]{1,0:T(8,128)(2,1)S(1)} %get-tuple-element.6.msa_ref, bf16[128,128]{1,0:T(8,128)(2,1)S(1)} %get-tuple-element.7.pair_ref), custom_call_target="tpu_custom_call" | custom-call | tf_op jit(solution)/shard_map/pallas_call | solution.py:463

commit v7 on v6

--- a/solution.py
+++ b/solution.py
@@ -50,9 +50,12 @@
     return lax.dot_general(a, b, (((0,), (0,)), ((), ())), preferred_element_type=F32)
 
 
-def softmax_rows(scores):
+def attend(stacked, keys, values, scale, bias, heads):
+    scores = matmul_nt(stacked, keys) * scale + bias
     exp_scores = jnp.exp(scores - jnp.max(scores, axis=-1, keepdims=True))
-    return (exp_scores * (1.0 / jnp.sum(exp_scores, axis=-1, keepdims=True))).astype(BF16)
+    total = jnp.sum(exp_scores, axis=-1, keepdims=True)
+    weighted = matmul(exp_scores.astype(BF16), values)
+    return head_merge(weighted, heads) / head_merge(jnp.broadcast_to(total, weighted.shape), heads)
 
 
 def head_stack(values, heads):
@@ -79,7 +82,7 @@
     out_msa, out_pair = refs[count : 2 + count]
     w = dict(zip(INPUTS, refs[2 + count : 2 + 2 * count]))
     (xg, pg, k_s, v_s, left_s, msg_s, gather, bias_s, pairin_s, tkv_s, wf_s, wp_s, opm_s,
-     flat_s, wsem, sx, rx, sp, rp, s1, r1, s2, r2) = refs[2 + 2 * count :]
+     flat_s, q_s, tq_s, wsem, sx, rx, sp, rp, s1, r1, s2, r2) = refs[2 + 2 * count :]
     x_ref, pair_ref = w["x"], w["pair"]
     rows_i, seqs, width = shape
     tiles = width // LANES
@@ -177,6 +180,8 @@
     loads["qkvg"].wait()
     proj = matmul(xn_own, w["qkvg"][...])
     query = proj[:, :width].astype(BF16).astype(F32)
+    for r in range(rows_i):
+        q_s[r] = head_stack(query[r * seqs : (r + 1) * seqs], VERTICAL_ATTENDS)
     gate = jax.nn.sigmoid(proj[:, 3 * width :].astype(BF16).astype(F32))
     k_s[p_me] = proj[:, width : 2 * width].astype(BF16)
     v_s[p_me] = proj[:, 2 * width : 3 * width].astype(BF16)
@@ -194,6 +199,8 @@
     tproj = matmul(pn_own, tri_w)
     tkv_s[p_me] = tproj[:, pwidth : 3 * pwidth].astype(BF16)
     tri_q = tproj[:, :pwidth].astype(BF16).astype(F32)
+    for i in range(rows_i):
+        tq_s[i] = head_stack(tri_q[i * cols : (i + 1) * cols], TRI_HEADS)
     tri_gate = jax.nn.sigmoid(tproj[:, 3 * pwidth :].astype(BF16).astype(F32))
     loads["tensor"].wait()
     wf_s[...] = w["tensor"][...].astype(F32)
@@ -257,13 +264,6 @@
     for _, copy in exchange:
         copy.start()
 
-    for slot in range(1, n_pb):
-        exchange[n_pb - slot - 1][0].wait_recv()
-    for d in range(1, n_pb):
-        p = (p_me + d) % n_pb
-        pn = normalize(pairin_s[p] + pg[d].astype(F32))
-        tkv_s[p] = matmul(pn, tri_w[:, pwidth : 3 * pwidth]).astype(BF16)
-
     second = []
     for a in range(n_as):
         slot = slot_of(a, b_me, c_me)
@@ -283,6 +283,13 @@
                 device_id=device(a_me, (b_me + db) % n_b, (c_me + dc) % n_c, p_me), device_id_type=MESH)
             copy.start()
             second.append(copy)
+
+    for slot in range(1, n_pb):
+        exchange[n_pb - slot - 1][0].wait_recv()
+    for d in range(1, n_pb):
+        p = (p_me + d) % n_pb
+        pn = normalize(pairin_s[p] + pg[d].astype(F32))
+        tkv_s[p] = matmul(pn, tri_w[:, pwidth : 3 * pwidth]).astype(BF16)
 
     for slot in range(1, n_pb):
         exchange[n_pb - slot - 1][1].wait_recv()
@@ -300,9 +307,8 @@
         span = slice(r * seqs, (r + 1) * seqs)
         keys = jnp.concatenate([k_s[p, span, :] for p in range(n_pb)], axis=0)
         values = jnp.concatenate([v_s[p, span, :] for p in range(n_pb)], axis=0)
-        scores = matmul_nt(head_stack(query[span], VERTICAL_ATTENDS), keys) * scale + seq_bias
-        weighted = matmul(softmax_rows(scores), values)
-        mixed.append((gate[span] * head_merge(weighted, VERTICAL_ATTENDS)).astype(BF16))
+        attended = attend(q_s[r], keys, values, scale, seq_bias, VERTICAL_ATTENDS)
+        mixed.append((gate[span] * attended).astype(BF16))
 
     loads["vproj"].wait()
     mid = x_own + matmul(jnp.concatenate(mixed, axis=0), w["vproj"][...])
@@ -360,9 +366,8 @@
         span = slice(i * cols, (i + 1) * cols)
         keys = jnp.concatenate([tkv_s[p, span, :pwidth] for p in range(n_pb)], axis=0)
         values = jnp.concatenate([tkv_s[p, span, pwidth:] for p in range(n_pb)], axis=0)
-        scores = matmul_nt(head_stack(tri_q[span], TRI_HEADS), keys) * scale + bias
-        weighted = matmul(softmax_rows(scores), values)
-        tri_mixed.append((tri_gate[span] * head_merge(weighted, TRI_HEADS)).astype(BF16))
+        attended = attend(tq_s[i], keys, values, scale, bias, TRI_HEADS)
+        tri_mixed.append((tri_gate[span] * attended).astype(BF16))
     loads["tout"].wait()
     pair_mid = pair_in + matmul(jnp.concatenate(tri_mixed, axis=0), w["tout"][...]) + opm
     loads["up"].wait()
@@ -444,6 +449,8 @@
             pltpu.VMEM(arrays["tensor"].shape, BF16),
             pltpu.VMEM((max(cells * SUBLANES, msg_rows), LANES), F32),
             pltpu.VMEM(arrays["x"].shape, F32),
+            pltpu.VMEM((rows_i, VERTICAL_ATTENDS * seqs, width), BF16),
+            pltpu.VMEM((rows_i, TRI_HEADS * cols, pwidth), BF16),
             dma((len(inputs),)),
             dma((n_pb,)),
             dma((n_pb,)),

time: 18.2 us -> 17.5 us (0.962)
  Pallas kernels: 17.4 us -> 16.7 us
    pallas_call x1, Pallas kernels: 16.7 us -> 16 us  [on_device(): pl.pallas_call(functools.partial(kernel, sizes, (rows_i, seqs, width)), o...]
where the time goes in v7:
time: 17.5 us; the launch traced here: 17.3 us
  Pallas kernels  16.7 us (95%)
  between operations  0.65 us (4%)
    pallas_call x1, Pallas kernels, on_device(): pl.pallas_call(functools.partial(kernel, sizes, (rows_i, seqs, width)), o...  16 us
    pallas_call x1, Pallas kernels, on_device(): pl.pallas_call(finish, out_shape=(jax.ShapeDtypeStruct(msa.shape, BF16),...  0.68 us

profile of v7, /device:TPU:0, one launch (start us, length us, event | category | flops | bytes accessed | tf_op | source)
XLA Modules:
  0.0 17.3 jit_solution(11218858445330548775)
XLA Ops:
  0.6 16.0 %shard_map.176 = (bf16[512,128]{1,0:T(8,128)(2,1)S(1)}, bf16[128,128]{1,0:T(8,128)(2,1)S(1)}) custom-call(bf16[512,128]{1,0:T(8,128)(2,1)} %bitcast.17, s32[1,128]{1,0:T(1,128)} %bitcast.22, bf16[64,256]{1,0:T(8,128)(2,1)} %bitcast.18, s32[1,64]{1,0:T(1,128)} %bitcast.20, s32[64]{0:T(128)} %refs_4_.1, bf16[65,128]{1,0:T(8,128)(2,1)} %refs_5_.1, ...), custom_call_target="tpu_custom_call" | custom-call | tf_op jit(solution)/shard_map/pallas_call | solution.py:426
  16.6 0.7 %shard_map.177 = (bf16[512,128]{1,0:T(8,128)(2,1)}, bf16[128,128]{1,0:T(8,128)(2,1)}) custom-call(bf16[512,128]{1,0:T(8,128)(2,1)S(1)} %get-tuple-element.6.msa_ref, bf16[128,128]{1,0:T(8,128)(2,1)S(1)} %get-tuple-element.7.pair_ref), custom_call_target="tpu_custom_call" | custom-call | tf_op jit(solution)/shard_map/pallas_call | solution.py:470

commit v8 on v7

--- a/solution.py
+++ b/solution.py
@@ -225,29 +225,6 @@
 
     pl.semaphore_wait(barrier, len(line) + len(mates))
 
-    p_to, a_slot = a_me // n_as, a_me % n_as
-    stays = p_to == p_me
-
-    def slot_of(a, b, c):
-        return (a * n_b + b) * n_c + c
-
-    def first(d):
-        return pltpu.make_async_remote_copy(
-            src_ref=msg_s, dst_ref=gather.at[slot_of(a_slot, b_me, c_me), p_me], send_sem=s1.at[d],
-            recv_sem=r1.at[a_slot * n_pb + p_me], device_id=device((a_me + d) % n_a, b_me, c_me, p_to),
-            device_id_type=MESH)
-
-    for d in range(1, n_a):
-        first(d).start()
-
-    @pl.when(jnp.logical_not(stays))
-    def _():
-        first(0).start()
-
-    @pl.when(stays)
-    def _():
-        gather[slot_of(a_slot, b_me, c_me), p_me] = msg_s[...]
-
     exchange = []
     for d in range(1, n_pb):
         peer = device(a_me, b_me, c_me, (p_me + d) % n_pb)
@@ -263,6 +240,29 @@
         copy.start()
     for _, copy in exchange:
         copy.start()
+
+    p_to, a_slot = a_me // n_as, a_me % n_as
+    stays = p_to == p_me
+
+    def slot_of(a, b, c):
+        return (a * n_b + b) * n_c + c
+
+    def first(d):
+        return pltpu.make_async_remote_copy(
+            src_ref=msg_s, dst_ref=gather.at[slot_of(a_slot, b_me, c_me), p_me], send_sem=s1.at[d],
+            recv_sem=r1.at[a_slot * n_pb + p_me], device_id=device((a_me + d) % n_a, b_me, c_me, p_to),
+            device_id_type=MESH)
+
+    for d in range(1, n_a):
+        first(d).start()
+
+    @pl.when(jnp.logical_not(stays))
+    def _():
+        first(0).start()
+
+    @pl.when(stays)
+    def _():
+        gather[slot_of(a_slot, b_me, c_me), p_me] = msg_s[...]
 
     second = []
     for a in range(n_as):

time: 17.5 us -> 19.6 us (1.12)
  Pallas kernels: 16.7 us -> 18.8 us
    pallas_call x1, Pallas kernels: 16 us -> 18.1 us  [on_device(): pl.pallas_call(functools.partial(kernel, sizes, (rows_i, seqs, width)), o...]
where the time goes in v8:
time: 19.6 us; the launch traced here: 19.4 us
  Pallas kernels  18.8 us (96%)
  between operations  0.65 us (3%)
    pallas_call x1, Pallas kernels, on_device(): pl.pallas_call(functools.partial(kernel, sizes, (rows_i, seqs, width)), o...  18.1 us
    pallas_call x1, Pallas kernels, on_device(): pl.pallas_call(finish, out_shape=(jax.ShapeDtypeStruct(msa.shape, BF16),...  0.68 us

profile of v8, /device:TPU:0, one launch (start us, length us, event | category | flops | bytes accessed | tf_op | source)
XLA Modules:
  0.0 19.4 jit_solution(15224887170643001666)
XLA Ops:
  0.6 18.1 %shard_map.176 = (bf16[512,128]{1,0:T(8,128)(2,1)S(1)}, bf16[128,128]{1,0:T(8,128)(2,1)S(1)}) custom-call(bf16[512,128]{1,0:T(8,128)(2,1)} %bitcast.17, s32[1,128]{1,0:T(1,128)} %bitcast.22, bf16[64,256]{1,0:T(8,128)(2,1)} %bitcast.18, s32[1,64]{1,0:T(1,128)} %bitcast.20, s32[64]{0:T(128)} %refs_4_.1, bf16[65,128]{1,0:T(8,128)(2,1)} %refs_5_.1, ...), custom_call_target="tpu_custom_call" | custom-call | tf_op jit(solution)/shard_map/pallas_call | solution.py:426
  18.7 0.7 %shard_map.177 = (bf16[512,128]{1,0:T(8,128)(2,1)}, bf16[128,128]{1,0:T(8,128)(2,1)}) custom-call(bf16[512,128]{1,0:T(8,128)(2,1)S(1)} %get-tuple-element.6.msa_ref, bf16[128,128]{1,0:T(8,128)(2,1)S(1)} %get-tuple-element.7.pair_ref), custom_call_target="tpu_custom_call" | custom-call | tf_op jit(solution)/shard_map/pallas_call | solution.py:470
